TPU v7x, 128 devices: a whole 4x4x4 slice. The times are simulated.
128 devices in a mesh: row: 8 (over y_lo, x), col: 16 (over z, y_hi, core).
Axes of the slice: x: 4, y: 4 (y_hi: 2, y_lo: 2; y = y_hi * 2 + y_lo), z: 4, core: 2. Of those that a mesh axis runs over, the one named last changes fastest.
Arguments:
- block_x: float32 [2048, 1024], P(('row', 'col'))
- tile_values: bfloat16 [8, 16, 1024, 4096], P('row', 'col')
- row_block: int32 [8, 16, 1024], P('row', 'col'), may hold values from 0 to 127, as said below
- col_block: int32 [8, 16, 1024], P('row', 'col'), may hold values from 0 to 255
- tile_counts: int32 [8, 16], P('row', 'col'), may hold values from 64 to 1024, as said below
Outputs:
- residual: float32 [2048, 1024], P(('row', 'col'))
- residual_image: float32 [2048, 1024], P(('row', 'col'))
- gram_small: float32 [16, 16], replicated
Inputs may be any that keep to these rules, and one draw needn't show every extreme that they name: In grid cell (r, c) the first 16 slots s hold row_block = r * 16 + s and col_block = c * 16 + s, the diagonal tiles of the cell's own vector blocks; slots at or past the count hold indices in range too. `tile_counts`: some grid cell uses all 1024 slots in every draw.
All inputs are finite; a program needn't handle non-finite values.
Results may differ from a plain program's by a relative error of at most 0.0096.
Values may be sent and summed in bfloat16 or wider, within the bound.
A program may use at most 128 MiB of HBM per device.

v0:
```python
import jax
import jax.numpy as jnp
from jax import lax
from jax.sharding import PartitionSpec as P

TILE = 64
K = 16


def gram_of(left, right):
    return jnp.einsum("bkj,blj->kl", left, right, precision=lax.Precision.HIGHEST)


def apply_hamiltonian(flat_half, square, rows_here, cols_here, live_mask):
    seg_rows = flat_half.shape[0]
    row_width = flat_half.shape[1]
    slot_count = square.shape[0]
    row_groups = lax.axis_size("row")
    col_groups = lax.axis_size("col")
    cols_all = lax.all_gather(flat_half, "col", axis=0, tiled=True)
    rows_all = lax.all_gather(flat_half, "row", axis=0, tiled=True)
    picked_cols = cols_all[cols_here].reshape(slot_count, K, TILE)
    forward = jnp.einsum("tkj,tij->tki", picked_cols, square, preferred_element_type=jnp.float32)
    forward = jnp.where(live_mask, forward.reshape(slot_count, row_width), 0.0)
    partial_rows = jax.ops.segment_sum(forward, rows_here, num_segments=row_groups * seg_rows)
    picked_rows = rows_all[rows_here].reshape(slot_count, K, TILE)
    backward = jnp.einsum("tki,tij->tkj", picked_rows, square, preferred_element_type=jnp.float32)
    backward = jnp.where(live_mask, backward.reshape(slot_count, row_width), 0.0)
    partial_cols = jax.ops.segment_sum(backward, cols_here, num_segments=col_groups * seg_rows)
    summed_rows = lax.psum(partial_rows, "row")
    along_rows = lax.dynamic_slice_in_dim(
        summed_rows, lax.axis_index("row") * seg_rows, seg_rows, 0
    )
    summed_cols = lax.psum(partial_cols, "col")
    along_cols = lax.dynamic_slice_in_dim(
        summed_cols, lax.axis_index("col") * seg_rows, seg_rows, 0
    )
    return along_rows + along_cols


def local(block_x, tile_values, row_block, col_block, tile_counts):
    seg_rows = block_x.shape[0]
    row_width = block_x.shape[1]
    slot_count = tile_values.shape[2]
    square = tile_values.reshape(slot_count, TILE, TILE)
    rows_here = row_block.reshape(slot_count)
    cols_here = col_block.reshape(slot_count)
    live_mask = (lax.iota(jnp.int32, slot_count) < tile_counts.reshape(()))[:, None]
    vectors = block_x.reshape(seg_rows, K, TILE)
    row_groups = lax.axis_size("row")
    col_groups = lax.axis_size("col")
    image_flat = apply_hamiltonian(
        block_x.astype(jnp.bfloat16), square, rows_here, cols_here, live_mask
    )
    image = image_flat.reshape(seg_rows, K, TILE)
    cross_gram, norm_gram = lax.psum(
        (gram_of(image, vectors), gram_of(vectors, vectors)), ("row", "col")
    )
    lower_factor = jnp.linalg.cholesky(norm_gram)
    halfway = lax.linalg.triangular_solve(lower_factor, cross_gram.T, left_side=True, lower=True)
    coupling_t = lax.linalg.triangular_solve(
        lower_factor, halfway, left_side=True, lower=True, transpose_a=True
    )
    residual = image - jnp.einsum(
        "lk,blj->bkj", coupling_t, vectors, precision=lax.Precision.HIGHEST
    )
    residual_flat = residual.reshape(seg_rows, row_width)
    back_flat = apply_hamiltonian(
        residual_flat.astype(jnp.bfloat16), square, rows_here, cols_here, live_mask
    )
    back_image = back_flat.reshape(seg_rows, K, TILE)
    total_rows = row_groups * col_groups * seg_rows * TILE
    gram_small = lax.psum(gram_of(residual, back_image), ("row", "col")) / total_rows
    return (residual_flat, back_flat, gram_small)


def solution(mesh):
    placed = (
        P(("row", "col"), None),
        P("row", "col", None, None),
        P("row", "col", None),
        P("row", "col", None),
        P("row", "col"),
    )
    return jax.shard_map(
        local,
        mesh=mesh,
        in_specs=placed,
        out_specs=(P(("row", "col"), None), P(("row", "col"), None), P()),
        check_vma=False,
    )
```

profile of v0, /device:TPU:1, one launch (start us, length us, event | category | flops | bytes accessed | tf_op | source)
XLA Modules:
  0.0 911.1 jit_solution(423037173320512852)
XLA Ops:
  7.2 0.8 convert_element_type.6
  8.1 29.2 %all_gather.12 = bf16[256,1024]{1,0:T(8,128)(2,1)S(1)} all-gather(bf16[16,1024]{1,0:T(8,128)(2,1)S(1)} %convert_element_type.6), channel_id=1, replica_groups=mesh['row'=8,'col'=16] {'col'}, dimensions={0}, use_global_device_ids=true | all-gather | bytes 557056 | tf_op jit(solution)/shard_map/all_gather | solution.py:20
  37.3 22.0 %all_gather.13 = bf16[128,1024]{1,0:T(8,128)(2,1)S(1)} all-gather(bf16[16,1024]{1,0:T(8,128)(2,1)S(1)} %convert_element_type.6), channel_id=1, replica_groups=mesh['row'=8,'col'=16] {'row'}, dimensions={0}, use_global_device_ids=true | all-gather | bytes 294912 | tf_op jit(solution)/shard_map/all_gather | solution.py:21
  59.3 12.0 %copy.11 = bf16[1,1,1024,4096]{2,3,1,0:T(8,128)(2,1)} copy(bf16[1,1,1024,4096]{3,2,1,0:T(8,128)(2,1)} %param.6) | data formatting | bytes 16777216 | tf_op args[1]
  71.3 23.9 %copy.13 = bf16[1024,64,64]{2,1,0:T(8,128)(2,1)} copy(bf16[1024,64,64]{0,2,1:T(8,128)(2,1)} %bitcast.64) | data formatting | bytes 16777216 | tf_op jit(solution)/shard_map/reshape | solution.py:45
  95.2 4.1 gather_fusion
  99.3 2.6 copy.10
  101.9 6.2 copy.12
  108.1 14.9 %fusion.14 = f32[1024,16,64]{2,1,0:T(8,128)} fusion(bf16[1024,16,64]{2,1,0:T(8,128)(2,1)} %copy.12, bf16[1024,64,64]{2,1,0:T(8,128)(2,1)} %copy.13), kind=kOutput, calls=%fused_computation.45 | convolution fusion | flops 134217728 | bytes 14680064 | tf_op jit(solution)/shard_map/tkj,tij->tki/dot_general | solution.py:23
  122.9 6.8 copy.14
  129.8 4.1 gather_fusion.1
  133.8 2.6 copy.16
  136.4 6.2 copy.17
  142.6 11.3 %fusion.15 = f32[1024,16,64]{2,1,0:T(8,128)} fusion(bf16[1024,16,64]{2,1,0:T(8,128)(2,1)} %copy.17, bf16[1024,64,64]{2,1,0:T(8,128)(2,1)} %copy.13), kind=kOutput, calls=%fused_computation.46 | convolution fusion | flops 134217728 | bytes 14680064 | tf_op jit(solution)/shard_map/tki,tij->tkj/dot_general | solution.py:27
  153.9 6.8 copy.19
  161.4 8.6 bitcast_select_fusion.3
  170.0 5.3 copy.15
  175.4 11.6 %scatter_custom_fusion = f32[128,1024]{1,0:T(8,128)} fusion(s32[1024]{0:T(1024)S(1)} %bitcast.71, f32[1024,1024]{1,0:T(8,128)} %copy.15, f32[]{:T(128)} %constant.59.clone.1), kind=kCustom, calls=%fused_computation.24 | custom fusion | flops 1048576 | bytes 524800 | tf_op jit(solution)/shard_map/scatter-add | solution.py:25
  187.0 0.0 all-reduce.8.cloned.1.call-start
  187.0 5.4 copy.20
  192.4 11.4 %scatter_custom_fusion.1 = f32[256,1024]{1,0:T(8,128)} fusion(s32[1024]{0:T(1024)S(1)} %bitcast.73, f32[1024,1024]{1,0:T(8,128)} %copy.20, f32[]{:T(128)} %constant.59.clone.1), kind=kCustom, calls=%fused_computation.20 | custom fusion | flops 1048576 | bytes 1049088 | tf_op jit(solution)/shard_map/scatter-add | solution.py:29
  203.8 0.0 all-reduce.10.cloned.1.call-start
  203.9 0.1 reshape.131
  203.9 0.2 convolution_bitcast_fusion.4
  204.2 54.7 %all-reduce.6.cloned.1.call-done = f32[128,1024]{1,0:T(8,128)} async-done(((f32[128,1024]{1,0:T(8,128)}), f32[128,1024]{1,0:T(8,128)}) %all-reduce.6.cloned.1.call-update) | async-done | bytes 524304 | tf_op jit(solution)/shard_map/psum | solution.py:30
  258.9 147.6 %all-reduce.8.cloned.1.call-done = f32[256,1024]{1,0:T(8,128)} async-done(((f32[256,1024]{1,0:T(8,128)}), f32[256,1024]{1,0:T(8,128)}) %all-reduce.8.cloned.1.call-update) | async-done | bytes 1048592 | tf_op jit(solution)/shard_map/psum | solution.py:34
  406.4 0.9 dynamic-slice_add_fusion.1
  407.3 0.1 reshape.130
  407.4 0.2 convolution_bitcast_fusion.3
  407.7 67.1 %all-reduce = (f32[16,16]{1,0:T(8,128)S(1)}, f32[16,16]{0,1:T(8,128)S(1)}) all-reduce(f32[16,16]{1,0:T(8,128)S(1)} %convolution_bitcast_fusion.3, f32[16,16]{0,1:T(8,128)S(1)} %convolution_bitcast_fusion.4), channel_id=1, replica_groups=mesh['row'=8,'col'=16] {'row','col'}, use_global_device_ids=true, to_apply=%region_7.8 | all-reduce | flops 512 | bytes 4096 | tf_op jit(solution)/shard_map/psum | solution.py:56
  474.8 0.1 copy.22
  474.9 1.5 cholesky.16
  476.3 0.6 compare_reduce_fusion
  477.0 0.6 fusion.9
  477.6 1.2 custom-call.8
  478.9 0.2 fusion.11
  479.1 0.2 convolution_bitcast_fusion.2
  479.3 0.3 fusion
  479.6 0.1 reshape.132
  479.7 22.1 %all_gather.15 = bf16[128,1024]{1,0:T(8,128)(2,1)S(1)} all-gather(bf16[16,1024]{1,0:T(8,128)(2,1)S(1)} %convert_element_type.7), channel_id=1, replica_groups=mesh['row'=8,'col'=16] {'row'}, dimensions={0}, use_global_device_ids=true | all-gather | bytes 294912 | tf_op jit(solution)/shard_map/all_gather | solution.py:21
  501.8 30.8 %all_gather.14 = bf16[256,1024]{1,0:T(8,128)(2,1)S(1)} all-gather(bf16[16,1024]{1,0:T(8,128)(2,1)S(1)} %convert_element_type.7), channel_id=1, replica_groups=mesh['row'=8,'col'=16] {'col'}, dimensions={0}, use_global_device_ids=true | all-gather | bytes 557056 | tf_op jit(solution)/shard_map/all_gather | solution.py:20
  532.6 4.2 gather_fusion.3
  536.9 2.6 copy.28
  539.5 6.2 copy.29
  545.6 11.3 %fusion.17 = f32[1024,16,64]{2,1,0:T(8,128)} fusion(bf16[1024,16,64]{2,1,0:T(8,128)(2,1)} %copy.29, bf16[1024,64,64]{2,1,0:T(8,128)(2,1)} %copy.13), kind=kOutput, calls=%fused_computation.48 | convolution fusion | flops 134217728 | bytes 14680064 | tf_op jit(solution)/shard_map/tki,tij->tkj/dot_general | solution.py:27
  556.9 6.8 copy.31
  563.7 4.1 gather_fusion.2
  567.8 2.6 copy.23
  570.4 6.2 copy.24
  576.6 14.9 %fusion.16 = f32[1024,16,64]{2,1,0:T(8,128)} fusion(bf16[1024,16,64]{2,1,0:T(8,128)(2,1)} %copy.24, bf16[1024,64,64]{2,1,0:T(8,128)(2,1)} %copy.13), kind=kOutput, calls=%fused_computation.47 | convolution fusion | flops 134217728 | bytes 14680064 | tf_op jit(solution)/shard_map/tkj,tij->tki/dot_general | solution.py:23
  591.4 6.9 copy.26
  598.3 8.6 bitcast_select_fusion.1
  606.9 5.3 copy.27
  612.3 11.4 %scatter_custom_fusion.2 = f32[128,1024]{1,0:T(8,128)} fusion(s32[1024]{0:T(1024)S(1)} %bitcast.72, f32[1024,1024]{1,0:T(8,128)} %copy.27, f32[]{:T(128)} %constant.59.clone.1), kind=kCustom, calls=%fused_computation.22 | custom fusion | flops 1048576 | bytes 524800 | tf_op jit(solution)/shard_map/scatter-add | solution.py:25
  623.7 0.0 all-reduce.12.cloned.1.call-start
  623.7 5.4 copy.32
  629.1 11.4 %scatter_custom_fusion.3 = f32[256,1024]{1,0:T(8,128)} fusion(s32[1024]{0:T(1024)S(1)} %bitcast.74, f32[1024,1024]{1,0:T(8,128)} %copy.32, f32[]{:T(128)} %constant.59.clone.1), kind=kCustom, calls=%fused_computation.18 | custom fusion | flops 1048576 | bytes 1049088 | tf_op jit(solution)/shard_map/scatter-add | solution.py:29
  640.5 47.7 %all-reduce.10.cloned.1.call-done = f32[128,1024]{1,0:T(8,128)} async-done(((f32[128,1024]{1,0:T(8,128)}), f32[128,1024]{1,0:T(8,128)}) %all-reduce.10.cloned.1.call-update) | async-done | bytes 524304 | tf_op jit(solution)/shard_map/psum | solution.py:30
  688.2 147.4 %all-reduce.12.cloned.1.call-done = f32[256,1024]{1,0:T(8,128)} async-done(((f32[256,1024]{1,0:T(8,128)}), f32[256,1024]{1,0:T(8,128)}) %all-reduce.12.cloned.1.call-update) | async-done | bytes 1048592 | tf_op jit(solution)/shard_map/psum | solution.py:34
  835.6 0.9 dynamic-slice_add_fusion
  836.5 0.1 reshape.137
  836.6 0.2 convolution_bitcast_fusion.1
  836.8 67.0 %psum.55 = f32[16,16]{1,0:T(8,128)S(1)} all-reduce(f32[16,16]{1,0:T(8,128)S(1)} %convolution_bitcast_fusion.1), channel_id=1, replica_groups=mesh['row'=8,'col'=16] {'row','col'}, use_global_device_ids=true, to_apply=%region_12.13 | all-reduce | flops 256 | bytes 2048 | tf_op jit(solution)/shard_map/psum | solution.py:73
  903.8 0.6 broadcast_multiply_fusion
  (23 shorter events, 0.2 us)
Async XLA Ops:
  7.2 251.7 %all-reduce.6.cloned.1.call-start = ((), (), s32[]{:S(2)}) async-start(), calls=%async_computation | async-start | bytes 1048576 | tf_op jit(solution)/shard_map/psum | solution.py:30
  71.3 23.9 %copy-start.4 = (s32[1,1,1024]{2,1,0:T(1,128)S(1)}, s32[1,1,1024]{2,1,0:T(1,128)}, u32[]{:S(2)}) copy-start(s32[1,1,1024]{2,1,0:T(1,128)} %param.8) | copy-start | bytes 12292
  122.9 6.8 copy-start.3
  187.0 219.5 %all-reduce.8.cloned.1.call-start = ((), (), s32[]{:S(2)}) async-start(), calls=%async_computation.1 | async-start | bytes 2097152 | tf_op jit(solution)/shard_map/psum | solution.py:34
  187.0 16.8 %copy-start.1 = (f32[16,1024]{1,0:T(8,128)S(1)}, f32[16,1024]{1,0:T(8,128)}, u32[]{:S(2)}) copy-start(f32[16,1024]{1,0:T(8,128)} %param.5) | copy-start | bytes 196612
  203.8 484.4 %all-reduce.10.cloned.1.call-start = ((), (), s32[]{:S(2)}) async-start(), calls=%async_computation.2 | async-start | bytes 1048576 | tf_op jit(solution)/shard_map/psum | solution.py:30
  479.7 57.2 %copy-start.2 = (f32[16,1024]{1,0:T(8,128)}, f32[16,1024]{1,0:T(8,128)S(1)}, u32[]{:S(2)}) copy-start(f32[16,1024]{1,0:T(8,128)S(1)} %reshape.132) | copy-start | bytes 196612
  623.7 211.9 %all-reduce.12.cloned.1.call-start = ((), (), s32[]{:S(2)}) async-start(), calls=%async_computation.3 | async-start | bytes 2097152 | tf_op jit(solution)/shard_map/psum | solution.py:34
  836.5 67.9 %copy-start = (f32[16,1024]{1,0:T(8,128)}, f32[16,1024]{1,0:T(8,128)S(1)}, u32[]{:S(2)}) copy-start(f32[16,1024]{1,0:T(8,128)S(1)} %dynamic-slice_add_fusion) | copy-start | bytes 196612
Sparse Core Ops, SparseCore 0:
  187.1 71.7 all-reduce.5
  261.5 144.8 all-reduce.7
  623.8 64.3 all-reduce.9
  690.7 144.8 all-reduce.11
where the time goes:
time: 922 us; the launch traced here: 911 us
  waiting for transfers between devices  397 us (43%)
  blocking collectives  238 us (26%)
  local copies, waits for them, and re-layouts  137 us (15%)
  other arithmetic  70.2 us (8%)
  matrix products  53.7 us (6%)
  between operations  14.8 us (2%)
    psum x2, waiting for transfers between devices, apply_hamiltonian(): summed_cols = lax.psum(partial_cols, 'col')  295 us
    psum x2, waiting for transfers between devices, apply_hamiltonian(): summed_rows = lax.psum(partial_rows, 'row')  102 us
    psum x1, blocking collectives, local(): lax.psum((gram_of(image, vectors), gram_of(vectors, vectors)), ('row', 'c...  67.1 us
    psum x1, blocking collectives, local(): lax.psum(gram_of(residual, back_image), ('row', 'col')) / total_rows  67 us
    all_gather x2, blocking collectives, apply_hamiltonian(): cols_all = lax.all_gather(flat_half, 'col', axis=0, tiled=True)  60.1 us
    all_gather x2, blocking collectives, apply_hamiltonian(): rows_all = lax.all_gather(flat_half, 'row', axis=0, tiled=True)  44.1 us
    dot_general x2, matrix products, apply_hamiltonian(): jnp.einsum('tkj,tij->tki', picked_cols, square, preferred_element_type=jn...  29.7 us
    reshape x1, local copies, waits for them, and re-layouts, local(): square = tile_values.reshape(slot_count, TILE, TILE)  23.9 us
  transfers between devices with their start and end apart: 4, of which 4 were waited for; matrix products, arithmetic and copies ran while one was open for 4% of the time, Pallas kernels for 0%

commit v1 on v0

v1 whole, which is shorter than its diff:
```python
import functools

import jax
import jax.numpy as jnp
from jax import lax
from jax.experimental import pallas as pl
from jax.experimental.pallas import tpu as pltpu
from jax.sharding import PartitionSpec as P

F32 = jnp.float32
BF16 = jnp.bfloat16
TILE = 64
K = 16
SEGB = 16
SLOTS = 1024
GROUPS = SLOTS // 4
WIDTH = K * TILE
N_ROW = 8
N_COL = 16
RB = N_ROW * SEGB
CB = N_COL * SEGB
STAGE_PITCH = 136
Y_PITCH = 520
HIGHEST = lax.Precision.HIGHEST
NT = (((1,), (1,)), ((), ()))
NN = (((1,), (0,)), ((), ()))


def left_half(rows):
    return lax.broadcasted_iota(jnp.int32, (rows, 128), 1) < TILE


def swap_halves(value):
    return pltpu.roll(value, TILE, 1)


def lane_block(index):
    start = index * 128
    if not isinstance(index, int):
        start = pl.multiple_of(start, 128)
    return pl.ds(start, 128)


def flat_to_by_vector(flat, temp, out):
    lt = left_half(8)

    def step(pair, carry):
        low = flat[0:8, lane_block(pair)]
        high = flat[8:16, lane_block(pair)]
        temp[pl.ds(2 * pair, 8, stride=K), :] = jnp.where(lt, low, swap_halves(high))
        temp[pl.ds(2 * pair + 1, 8, stride=K), :] = jnp.where(lt, swap_halves(low), high)
        return carry

    lax.fori_loop(0, K // 2, step, 0, unroll=True)
    gather_blocks(temp, out)


def gather_blocks(temp, out):
    def step(p, carry):
        out[:, lane_block(p)] = temp[pl.ds(pl.multiple_of(p * K, K), K), :]
        return carry

    lax.fori_loop(0, 8, step, 0, unroll=True)


def by_row_to_by_vector(by_row, temp, out):
    def step(k, carry):
        temp[pl.ds(k, 8, stride=K), :] = by_row[pl.ds(pl.multiple_of(k * 8, 8), 8), :]
        return carry

    lax.fori_loop(0, K, step, 0, unroll=True)
    gather_blocks(temp, out)


def by_vector_to_by_row(by_vector, temp, out):
    def spread(p, carry):
        temp[pl.ds(pl.multiple_of(p * K, K), K), :] = by_vector[:, lane_block(p)]
        return carry

    def collect(k, carry):
        out[pl.ds(pl.multiple_of(k * 8, 8), 8), :] = temp[pl.ds(k, 8, stride=K), :]
        return carry

    lax.fori_loop(0, 8, spread, 0, unroll=True)
    lax.fori_loop(0, K, collect, 0, unroll=True)


def by_row_to_flat(by_row, flat):
    lt = left_half(8)

    def step(pair, carry):
        even = by_row[pl.ds(pl.multiple_of(pair * 16, 8), 8), :]
        odd = by_row[pl.ds(pl.multiple_of(pair * 16 + 8, 8), 8), :]
        flat[0:8, lane_block(pair)] = jnp.where(lt, even, swap_halves(odd))
        flat[8:16, lane_block(pair)] = jnp.where(lt, swap_halves(even), odd)
        return carry

    lax.fori_loop(0, K // 2, step, 0, unroll=True)


def load_groups(raw, stage, tiles, chunk, count):
    lt = left_half(16)
    lane_row = lax.broadcasted_iota(jnp.int32, (16, 128), 0)

    def half(a, carry):
        live = [lane_row + ((2 * a + b) * GROUPS + chunk * 16) < count for b in range(2)]

        def step(m, inner):
            first = jnp.where(live[0], raw[chunk, 2 * a, :, lane_block(m)].astype(F32), 0.0)
            second = jnp.where(live[1], raw[chunk, 2 * a + 1, :, lane_block(m)].astype(F32), 0.0)
            even = jnp.where(lt, first, swap_halves(second))
            odd = jnp.where(lt, swap_halves(first), second)
            for h in range(2):
                base = h * 8 * STAGE_PITCH + a * TILE + 2 * m
                stage[pl.ds(base, 8, stride=STAGE_PITCH), :] = even[h * 8 : h * 8 + 8]
                stage[pl.ds(base + 1, 8, stride=STAGE_PITCH), :] = odd[h * 8 : h * 8 + 8]
            return inner

        return lax.fori_loop(0, 32, step, carry, unroll=True)

    lax.fori_loop(0, 2, half, 0, unroll=True)

    def narrow(u, carry):
        tiles[chunk * 16 + u] = stage[pl.ds(pl.multiple_of(u * STAGE_PITCH, 8), 128), :].astype(BF16)
        return carry

    lax.fori_loop(0, 16, narrow, 0, unroll=True)


def fill_table(own, table, base):
    lt = left_half(16)
    zero = jnp.zeros((16, 128), BF16)

    def step(p, carry):
        both = own[:, lane_block(p)]
        turned = swap_halves(both)
        table[base + p, 0] = jnp.where(lt, both, zero)
        table[base + p, 1] = jnp.where(lt, zero, turned)
        table[base + 8 + p, 0] = jnp.where(lt, turned, zero)
        table[base + 8 + p, 1] = jnp.where(lt, zero, both)
        return carry

    lax.fori_loop(0, 8, step, 0, unroll=True)


def multiply(index, table, tiles, products, forward, turned=None):
    lt = left_half(16)

    def step(q, carry):
        picked = [table[index[0, 0, g * GROUPS + q], (g % 2) if forward else (g // 2)] for g in range(4)]
        left = jnp.concatenate(picked, axis=0)
        matrix = tiles[q]
        if turned is not None:
            turned[q] = matrix.T
        out = lax.dot_general(left, matrix, NN, preferred_element_type=F32)
        for s in range(2):
            one, two = (s, 2 + s) if forward else (2 * s, 2 * s + 1)
            merged = jnp.where(lt, out[one * 16 : one * 16 + 16], out[two * 16 : two * 16 + 16])
            place = s * GROUPS + q
            products[pl.ds(place, 8, stride=Y_PITCH), :] = merged[:8]
            products[pl.ds(8 * Y_PITCH + place, 8, stride=Y_PITCH), :] = merged[8:]
        return carry

    lax.fori_loop(0, GROUPS, step, 0, unroll=64)


def add_up(places, products, out, blocks):
    lt = left_half(8)

    def step(pair, carry):
        part = [
            products[pl.ds(pl.multiple_of((2 * pair + i) * Y_PITCH, 8), SLOTS // 2), :].astype(BF16) for i in range(2)
        ]
        total = jnp.dot(places[...], jnp.concatenate(part, axis=1), preferred_element_type=F32)
        for target in range(blocks // SEGB):
            rows = []
            for i in range(2):
                half = []
                for h in range(2):
                    first = target * SEGB + h * 8
                    left = total[first : first + 8, i * 128 : i * 128 + 128]
                    right = total[blocks + first : blocks + first + 8, i * 128 : i * 128 + 128]
                    both = jnp.where(lt, left, right)
                    half.append(both + swap_halves(both))
                rows.append(jnp.where(lt, half[0], half[1]))
            out[target, pl.ds(pl.multiple_of(pair * 16, 16), 16), :] = jnp.concatenate(rows, axis=0).astype(BF16)
        return carry

    lax.fori_loop(0, K // 2, step, 0, unroll=True)


def factor(norm):
    row = lax.broadcasted_iota(jnp.int32, (K, K), 0)
    lane = lax.broadcasted_iota(jnp.int32, (K, K), 1)

    def step(j, carry):
        matrix, inverse = carry
        pivot_row = jnp.sum(jnp.where(row == j, matrix, 0.0), axis=0, keepdims=True)
        pivot_inv = jnp.sum(jnp.where(row == j, inverse, 0.0), axis=0, keepdims=True)
        column = jnp.sum(jnp.where(lane == j, matrix, 0.0), axis=1, keepdims=True)
        pivot = jnp.sum(jnp.where((lane == j) & (row == j), matrix, 0.0), keepdims=True)
        scale = jnp.where(row[:, 0:1] > j, column / pivot, 0.0)
        return matrix - scale * pivot_row, inverse - scale * pivot_inv

    start = (norm, jnp.where(row == lane, 1.0, 0.0).astype(F32))
    matrix, inverse = lax.fori_loop(0, K, step, start)
    diagonal = jnp.sum(jnp.where(row == lane, matrix, 0.0), axis=1, keepdims=True)
    return inverse, 1.0 / diagonal


def kernel(
    block_x, tile_values, row_s, col_s, count_s, row_v, col_v,
    residual_out, image_out, gram_out,
    raw, stage, tiles, turned, table_r, table_c, place_r, place_c, prod_r, prod_c,
    temp, by_row, vec_x, vec_a, vec_b, own, got_r, got_c, part_r, part_c, sum_r, sum_c, gram_own, gram_r, gram_c,
    load_sem, send_r, send_c, recv_r, recv_c,
):
    my_row, my_col = lax.axis_index("row"), lax.axis_index("col")
    axes = {"row": (N_ROW, my_row, send_r, recv_r), "col": (N_COL, my_col, send_c, recv_c)}

    def copy(axis, kind, source, target, slot, peer):
        size, me, send, recv = axes[axis]
        return pltpu.make_async_remote_copy(
            src_ref=source, dst_ref=target, send_sem=send.at[kind, peer], recv_sem=recv.at[kind, slot],
            device_id={axis: peer}, device_id_type=pl.DeviceIdType.MESH,
        )

    def send_all(axis, kind, source_of, buffer):
        size, me, _, _ = axes[axis]

        def step(d, carry):
            peer = lax.rem(me + d, size)
            copy(axis, kind, source_of(peer), buffer.at[me], me, peer).start()
            return carry

        lax.fori_loop(1, size, step, 0)

    def finish_sends(axis, kind, source_of, buffer):
        size, me, _, _ = axes[axis]

        def step(d, carry):
            peer = lax.rem(me + d, size)
            copy(axis, kind, source_of(peer), buffer.at[me], me, peer).wait_send()
            return carry

        lax.fori_loop(1, size, step, 0)

    def each_arrival(axis, kind, source_of, buffer, use, start=0):
        size, me, _, _ = axes[axis]

        def step(d, carry):
            slot = lax.rem(me + size - d, size)
            copy(axis, kind, source_of(slot), buffer.at[slot], slot, slot).wait_recv()
            return use(slot, carry)

        return lax.fori_loop(1, size, step, start)

    def load(chunk, g):
        return pltpu.make_async_copy(
            tile_values.at[0, 0, pl.ds(pl.multiple_of(g * GROUPS + chunk * 16, 16), 16), :],
            raw.at[chunk, g], load_sem.at[chunk, g],
        )

    def start_load(chunk, carry):
        for g in range(4):
            load(chunk, g).start()
        return carry

    lax.fori_loop(0, SLOTS // 64, start_load, 0)
    barrier = pltpu.get_barrier_semaphore()
    for axis in ("row", "col"):
        size, me, _, _ = axes[axis]

        def greet(d, carry, axis=axis, size=size, me=me):
            pl.semaphore_signal(
                barrier, inc=1, device_id={axis: lax.rem(me + d, size)}, device_id_type=pl.DeviceIdType.MESH
            )
            return carry

        lax.fori_loop(1, size, greet, 0)

    flat_to_by_vector(block_x, temp, vec_x)
    own[0] = vec_x[...].astype(BF16)
    norm = lax.dot_general(vec_x[...], vec_x[...], NT, precision=HIGHEST, preferred_element_type=F32)
    gram_own[0] = jnp.zeros((K, 128), F32)
    gram_own[0, :, 0:K] = norm

    pl.semaphore_wait(barrier, N_ROW + N_COL - 2)

    def gather(step):
        source = lambda peer: own.at[step]
        send_all("row", step, source, got_r.at[step])
        send_all("col", step, source, got_c.at[step])

    def gram_row(which):
        source = lambda peer: gram_own.at[which]
        send_all("row", 4 + which, source, gram_r.at[which])
        gram_r[which, my_row] = gram_own[which]

    def gram_col(which):
        each_arrival("row", 4 + which, lambda s: gram_own.at[which], gram_r.at[which], lambda s, c: c)
        gram_own[3 + which] = jnp.sum(gram_r[which], axis=0)
        source = lambda peer: gram_own.at[3 + which]
        send_all("col", 4 + which, source, gram_c.at[which])
        gram_c[which, my_col] = gram_own[3 + which]

    def gram_done(which):
        each_arrival("col", 4 + which, lambda s: gram_own.at[3 + which], gram_c.at[which], lambda s, c: c)
        return jnp.sum(gram_c[which], axis=0)[:, 0:K]

    gather(0)
    gram_row(0)

    count = count_s[0, 0]

    def arrange(chunk, carry):
        for g in range(4):
            load(chunk, g).wait()
        load_groups(raw, stage, tiles, chunk, count)
        return carry

    lax.fori_loop(0, SLOTS // 64, arrange, 0)
    for s in range(2):
        columns = jnp.concatenate(
            [col_v[0, :, s * 256 : s * 256 + 256], col_v[0, :, 512 + s * 256 : 768 + s * 256]], axis=1
        )
        hit = lax.broadcasted_iota(jnp.int32, (CB, 512), 0) == columns
        place_c[s * CB : s * CB + CB, :] = jnp.where(hit, 1.0, 0.0).astype(BF16)
        hit = lax.broadcasted_iota(jnp.int32, (RB, 512), 0) == row_v[0, :, s * 512 : s * 512 + 512]
        place_r[s * RB : s * RB + RB, :] = jnp.where(hit, 1.0, 0.0).astype(BF16)
    gram_col(0)

    def product(step, while_waiting):
        source = lambda s: own.at[step]

        def enter(buffer, table):
            def use(slot, carry):
                fill_table(buffer.at[step, slot], table, slot * SEGB)
                return carry

            return use

        fill_table(own.at[step], table_r, my_row * SEGB)
        each_arrival("row", step, source, got_r.at[step], enter(got_r, table_r))
        multiply(row_s, table_r, tiles, prod_c, False, turned if step == 0 else None)
        add_up(place_c, prod_c, part_c.at[step], CB)
        send_all("col", 2 + step, lambda peer: part_c.at[step, peer], sum_c.at[step])
        fill_table(own.at[step], table_c, my_col * SEGB)
        each_arrival("col", step, source, got_c.at[step], enter(got_c, table_c))
        multiply(col_s, table_c, turned, prod_r, True)
        add_up(place_r, prod_r, part_r.at[step], RB)
        send_all("row", 2 + step, lambda peer: part_r.at[step, peer], sum_r.at[step])
        extra = while_waiting()
        total = part_c[step, my_col].astype(F32) + part_r[step, my_row].astype(F32)

        def add(buffer):
            return lambda slot, carry: carry + buffer[step, slot].astype(F32)

        total = each_arrival("col", 2 + step, lambda s: part_c.at[step, s], sum_c.at[step], add(sum_c), total)
        total = each_arrival("row", 2 + step, lambda s: part_r.at[step, s], sum_r.at[step], add(sum_r), total)
        by_row[...] = total
        return extra

    inverse, scale = product(0, lambda: factor(gram_done(0)))
    by_row_to_by_vector(by_row, temp, vec_a)
    gram_own[1] = jnp.zeros((K, 128), F32)
    gram_own[1, :, 0:K] = lax.dot_general(vec_a[...], vec_x[...], NT, precision=HIGHEST, preferred_element_type=F32)
    gram_row(1)
    gram_col(1)
    cross = gram_done(1)
    halfway = lax.dot_general(inverse, cross, NT, precision=HIGHEST, preferred_element_type=F32) * scale
    coupling = lax.dot_general(
        halfway, inverse, (((0,), (0,)), ((), ())), precision=HIGHEST, preferred_element_type=F32
    )
    vec_a[...] = vec_a[...] - jnp.dot(coupling, vec_x[...], precision=HIGHEST, preferred_element_type=F32)
    own[1] = vec_a[...].astype(BF16)
    gather(1)
    by_vector_to_by_row(vec_a, temp, by_row)
    by_row_to_flat(by_row, residual_out)

    product(1, lambda: None)
    by_row_to_by_vector(by_row, temp, vec_b)
    gram_own[2] = jnp.zeros((K, 128), F32)
    gram_own[2, :, 0:K] = lax.dot_general(vec_a[...], vec_b[...], NT, precision=HIGHEST, preferred_element_type=F32)
    gram_row(2)
    by_row_to_flat(by_row, image_out)
    gram_col(2)
    gram_out[...] = gram_done(2) * (1.0 / (N_ROW * N_COL * SEGB * TILE))

    for step in range(2):
        source = lambda peer, step=step: own.at[step]
        finish_sends("row", step, source, got_r.at[step])
        finish_sends("col", step, source, got_c.at[step])
        finish_sends("row", 2 + step, lambda peer, step=step: part_r.at[step, peer], sum_r.at[step])
        finish_sends("col", 2 + step, lambda peer, step=step: part_c.at[step, peer], sum_c.at[step])
    for which in range(3):
        finish_sends("row", 4 + which, lambda peer, which=which: gram_own.at[which], gram_r.at[which])
        finish_sends("col", 4 + which, lambda peer, which=which: gram_own.at[3 + which], gram_c.at[which])


def local(block_x, tile_values, row_block, col_block, tile_counts):
    vmem = pl.BlockSpec(memory_space=pltpu.VMEM)
    smem = pl.BlockSpec(memory_space=pltpu.SMEM)
    kinds = 7
    return pl.pallas_call(
        kernel,
        out_shape=(
            jax.ShapeDtypeStruct((SEGB, WIDTH), F32),
            jax.ShapeDtypeStruct((SEGB, WIDTH), F32),
            jax.ShapeDtypeStruct((K, K), F32),
        ),
        in_specs=[vmem, pl.BlockSpec(memory_space=pl.ANY), smem, smem, smem, vmem, vmem],
        out_specs=(vmem, vmem, vmem),
        scratch_shapes=[
            pltpu.VMEM((SLOTS // 64, 4, 16, TILE * TILE), BF16),
            pltpu.VMEM((16 * STAGE_PITCH, 128), F32),
            pltpu.VMEM((GROUPS, 128, 128), BF16),
            pltpu.VMEM((GROUPS, 128, 128), BF16),
            pltpu.VMEM((RB, 2, K, 128), BF16),
            pltpu.VMEM((CB, 2, K, 128), BF16),
            pltpu.VMEM((2 * RB, 512), BF16),
            pltpu.VMEM((2 * CB, 512), BF16),
            pltpu.VMEM((K * Y_PITCH, 128), F32),
            pltpu.VMEM((K * Y_PITCH, 128), F32),
            pltpu.VMEM((128, 128), F32),
            pltpu.VMEM((128, 128), F32),
            pltpu.VMEM((K, WIDTH), F32),
            pltpu.VMEM((K, WIDTH), F32),
            pltpu.VMEM((K, WIDTH), F32),
            pltpu.VMEM((2, K, WIDTH), BF16),
            pltpu.VMEM((2, N_ROW, K, WIDTH), BF16),
            pltpu.VMEM((2, N_COL, K, WIDTH), BF16),
            pltpu.VMEM((2, N_ROW, 128, 128), BF16),
            pltpu.VMEM((2, N_COL, 128, 128), BF16),
            pltpu.VMEM((2, N_ROW, 128, 128), BF16),
            pltpu.VMEM((2, N_COL, 128, 128), BF16),
            pltpu.VMEM((6, K, 128), F32),
            pltpu.VMEM((3, N_ROW, K, 128), F32),
            pltpu.VMEM((3, N_COL, K, 128), F32),
            pltpu.SemaphoreType.DMA((SLOTS // 64, 4)),
            pltpu.SemaphoreType.DMA((kinds, N_ROW)),
            pltpu.SemaphoreType.DMA((kinds, N_COL)),
            pltpu.SemaphoreType.DMA((kinds, N_ROW)),
            pltpu.SemaphoreType.DMA((kinds, N_COL)),
        ],
        compiler_params=pltpu.CompilerParams(
            collective_id=0, has_side_effects=True, vmem_limit_bytes=58 << 20
        ),
        cost_estimate=pl.CostEstimate(flops=1 << 30, bytes_accessed=9 << 20, transcendentals=0),
    )(block_x, tile_values, row_block, col_block, tile_counts, row_block, col_block)


def solution(mesh):
    placed = (
        P(("row", "col"), None),
        P("row", "col", None, None),
        P("row", "col", None),
        P("row", "col", None),
        P("row", "col"),
    )
    return jax.shard_map(
        local,
        mesh=mesh,
        in_specs=placed,
        out_specs=(P(("row", "col"), None), P(("row", "col"), None), P()),
        check_vma=False,
    )
```

time: 922 us -> 89.1 us (0.10); the launches traced: 911 us -> 88.8 us
  waiting for transfers between devices: 397 us -> 0 us
  blocking collectives: 238 us -> 0 us
  local copies, waits for them, and re-layouts: 137 us -> 4.24 us
  Pallas kernels: 0 us -> 83.2 us
  other arithmetic: 70.2 us -> 0 us
  matrix products: 53.7 us -> 0 us
  between operations: 14.8 us -> 1.29 us
    psum x4 -> x0, waiting for transfers between devices: 397 us -> none  [the longest x2 295 us: apply_hamiltonian(): summed_cols = lax.psum(partial_cols, 'col')]
    psum x2 -> x0, blocking collectives: 134 us -> none  [the longest x1 67.1 us: local(): lax.psum((gram_of(image, vectors), gram_of(vectors, vectors)), ('row', 'c...]
    all_gather x4 -> x0, blocking collectives: 104 us -> none  [the longest x2 60.1 us: apply_hamiltonian(): cols_all = lax.all_gather(flat_half, 'col', axis=0, tiled=True)]
    pallas_call x0 -> x1, Pallas kernels: none -> 83.2 us  [local(): pl.pallas_call(kernel, out_shape=(jax.ShapeDtypeStruct((SEGB, WIDTH), F32...]
    dot_general x8 -> x0, matrix products: 53.3 us -> none  [the longest x2 29.7 us: apply_hamiltonian(): jnp.einsum('tkj,tij->tki', picked_cols, square, preferred_element_type=jn...]
    reshape x9 -> x0, local copies, waits for them, and re-layouts: 49 us -> none  [the longest x1 23.9 us: local(): square = tile_values.reshape(slot_count, TILE, TILE)]
    scatter-add x4 -> x0, other arithmetic: 45.6 us -> none  [the longest x2 22.9 us: apply_hamiltonian(): jax.ops.segment_sum(forward, rows_here, num_segments=row_groups * seg_rows)]
    dot_general x4 -> x0, local copies, waits for them, and re-layouts: 27.4 us -> none  [the longest x2 13.7 us: apply_hamiltonian(): jnp.einsum('tkj,tij->tki', picked_cols, square, preferred_element_type=jn...]
  transfers between devices with their start and end apart: 4 -> 0, of which waited for: 4 -> 0; matrix products, arithmetic and copies ran while one was open for 4% -> 0% of each run, Pallas kernels for 0% -> 0%
where the time goes in v1:
time: 89.1 us; the launch traced here: 88.8 us
  Pallas kernels  83.2 us (93%)
  local copies, waits for them, and re-layouts  4.24 us (5%)
  between operations  1.29 us (1%)
    pallas_call x1, Pallas kernels, local(): pl.pallas_call(kernel, out_shape=(jax.ShapeDtypeStruct((SEGB, WIDTH), F32...  83.2 us
    unnamed x3, local copies, waits for them, and re-layouts  4.24 us

profile of v1, /device:TPU:1, one launch (start us, length us, event | category | flops | bytes accessed | tf_op | source)
XLA Modules:
  0.0 88.8 jit_solution(8765075874589694865)
XLA Ops:
  1.3 83.2 %shard_map.76 = (f32[16,1024]{1,0:T(8,128)}, f32[16,1024]{1,0:T(8,128)}, f32[16,16]{1,0:T(8,128)}) custom-call(f32[16,1024]{1,0:T(8,128)} %block_x.1, bf16[1,1,1024,4096]{3,2,1,0:T(8,128)(2,1)} %tile_values.1, s32[1,1,1024]{2,1,0:T(1,128)} %row_v.1, s32[1,1,1024]{2,1,0:T(1,128)} %col_v.1, s32[1,1]{1,0:T(1,128)S(6)} %copy.11.count_s, s32[1,1,1024]{2,1,0:T(1,128)} %row_v.1, ...), custom_call_target="tpu_custom_call" | custom-call | flops 1073741824 | bytes 9437184 | tf_op jit(solution)/shard_map/pallas_call | solution.py:405
  84.5 1.5 %copy.12 = f32[16,1024]{1,0:T(8,128)} copy(f32[16,1024]{1,0:T(8,128)} %get-tuple-element.6) | data formatting | bytes 131072
  86.0 1.5 %copy.13 = f32[16,1024]{1,0:T(8,128)} copy(f32[16,1024]{1,0:T(8,128)} %get-tuple-element.7) | data formatting | bytes 131072
  87.5 1.3 %copy.14 = f32[16,16]{1,0:T(8,128)} copy(f32[16,16]{1,0:T(8,128)} %get-tuple-element.8) | data formatting | bytes 2048

commit v2 on v1

--- a/solution.py
+++ b/solution.py
@@ -21,6 +21,7 @@
 CB = N_COL * SEGB
 STAGE_PITCH = 136
 Y_PITCH = 520
+EARLY_CHUNKS = 8
 HIGHEST = lax.Precision.HIGHEST
 NT = (((1,), (1,)), ((), ()))
 NN = (((1,), (0,)), ((), ()))
@@ -61,15 +62,6 @@
         return carry
 
     lax.fori_loop(0, 8, step, 0, unroll=True)
-
-
-def by_row_to_by_vector(by_row, temp, out):
-    def step(k, carry):
-        temp[pl.ds(k, 8, stride=K), :] = by_row[pl.ds(pl.multiple_of(k * 8, 8), 8), :]
-        return carry
-
-    lax.fori_loop(0, K, step, 0, unroll=True)
-    gather_blocks(temp, out)
 
 
 def by_vector_to_by_row(by_vector, temp, out):
@@ -164,16 +156,16 @@
     lax.fori_loop(0, GROUPS, step, 0, unroll=64)
 
 
-def add_up(places, products, out, blocks):
+def add_up(places, products, temp, out, blocks):
     lt = left_half(8)
+    targets = blocks // SEGB
 
     def step(pair, carry):
         part = [
             products[pl.ds(pl.multiple_of((2 * pair + i) * Y_PITCH, 8), SLOTS // 2), :].astype(BF16) for i in range(2)
         ]
         total = jnp.dot(places[...], jnp.concatenate(part, axis=1), preferred_element_type=F32)
-        for target in range(blocks // SEGB):
-            rows = []
+        for target in range(targets):
             for i in range(2):
                 half = []
                 for h in range(2):
@@ -182,11 +174,18 @@
                     right = total[blocks + first : blocks + first + 8, i * 128 : i * 128 + 128]
                     both = jnp.where(lt, left, right)
                     half.append(both + swap_halves(both))
-                rows.append(jnp.where(lt, half[0], half[1]))
-            out[target, pl.ds(pl.multiple_of(pair * 16, 16), 16), :] = jnp.concatenate(rows, axis=0).astype(BF16)
+                temp[pl.ds(target * 128 + 2 * pair + i, 8, stride=K), :] = jnp.where(lt, half[0], half[1])
         return carry
 
     lax.fori_loop(0, K // 2, step, 0, unroll=True)
+
+    def narrow(target, carry):
+        for p in range(8):
+            rows = pl.ds(pl.multiple_of(target * 128 + p * K, K), K)
+            out[target, :, p * 128 : p * 128 + 128] = temp[rows, :].astype(BF16)
+        return carry
+
+    lax.fori_loop(0, targets, narrow, 0, unroll=True)
 
 
 def factor(norm):
@@ -212,45 +211,40 @@
     block_x, tile_values, row_s, col_s, count_s, row_v, col_v,
     residual_out, image_out, gram_out,
     raw, stage, tiles, turned, table_r, table_c, place_r, place_c, prod_r, prod_c,
-    temp, by_row, vec_x, vec_a, vec_b, own, got_r, got_c, part_r, part_c, sum_r, sum_c, gram_own, gram_r, gram_c,
-    load_sem, send_r, send_c, recv_r, recv_c,
+    temp, vec_x, vec_a, own, got_r, got_c, part_r, part_c, sum_r, sum_c, gram_own, gram_r, gram_c,
+    load_sem, send_r, send_c, recv_r, recv_c, gram_recv_r, gram_recv_c,
 ):
     my_row, my_col = lax.axis_index("row"), lax.axis_index("col")
-    axes = {"row": (N_ROW, my_row, send_r, recv_r), "col": (N_COL, my_col, send_c, recv_c)}
-
-    def copy(axis, kind, source, target, slot, peer):
-        size, me, send, recv = axes[axis]
-        return pltpu.make_async_remote_copy(
-            src_ref=source, dst_ref=target, send_sem=send.at[kind, peer], recv_sem=recv.at[kind, slot],
-            device_id={axis: peer}, device_id_type=pl.DeviceIdType.MESH,
-        )
+    size_of = {"row": N_ROW, "col": N_COL}
+    me_of = {"row": my_row, "col": my_col}
+    send_of = {"row": send_r, "col": send_c}
+    recv_of = {"row": recv_r, "col": recv_c}
+    gram_recv_of = {"row": gram_recv_r, "col": gram_recv_c}
 
     def send_all(axis, kind, source_of, buffer):
-        size, me, _, _ = axes[axis]
+        size, me = size_of[axis], me_of[axis]
+        arrived = recv_of[axis].at[kind, me] if kind < 4 else gram_recv_of[axis].at[kind - 4]
 
         def step(d, carry):
             peer = lax.rem(me + d, size)
-            copy(axis, kind, source_of(peer), buffer.at[me], me, peer).start()
+            pltpu.make_async_remote_copy(
+                src_ref=source_of(peer), dst_ref=buffer.at[me], send_sem=send_of[axis].at[kind], recv_sem=arrived,
+                device_id={axis: peer}, device_id_type=pl.DeviceIdType.MESH,
+            ).start()
             return carry
 
         lax.fori_loop(1, size, step, 0)
 
-    def finish_sends(axis, kind, source_of, buffer):
-        size, me, _, _ = axes[axis]
-
-        def step(d, carry):
-            peer = lax.rem(me + d, size)
-            copy(axis, kind, source_of(peer), buffer.at[me], me, peer).wait_send()
-            return carry
-
-        lax.fori_loop(1, size, step, 0)
-
-    def each_arrival(axis, kind, source_of, buffer, use, start=0):
-        size, me, _, _ = axes[axis]
+    def wait_bytes(buffer, axis, sem):
+        block = buffer.at[pl.ds(0, size_of[axis] - 1)]
+        pltpu.make_async_copy(block, block, sem).wait()
+
+    def each_arrival(axis, kind, buffer, use, start=0):
+        size, me = size_of[axis], me_of[axis]
 
         def step(d, carry):
             slot = lax.rem(me + size - d, size)
-            copy(axis, kind, source_of(slot), buffer.at[slot], slot, slot).wait_recv()
+            pltpu.make_async_copy(buffer.at[slot], buffer.at[slot], recv_of[axis].at[kind, slot]).wait()
             return use(slot, carry)
 
         return lax.fori_loop(1, size, step, start)
@@ -266,51 +260,24 @@
             load(chunk, g).start()
         return carry
 
-    lax.fori_loop(0, SLOTS // 64, start_load, 0)
     barrier = pltpu.get_barrier_semaphore()
     for axis in ("row", "col"):
-        size, me, _, _ = axes[axis]
-
-        def greet(d, carry, axis=axis, size=size, me=me):
+
+        def greet(d, carry, axis=axis):
             pl.semaphore_signal(
-                barrier, inc=1, device_id={axis: lax.rem(me + d, size)}, device_id_type=pl.DeviceIdType.MESH
+                barrier, inc=1, device_id={axis: lax.rem(me_of[axis] + d, size_of[axis])},
+                device_id_type=pl.DeviceIdType.MESH,
             )
             return carry
 
-        lax.fori_loop(1, size, greet, 0)
-
+        lax.fori_loop(1, size_of[axis], greet, 0)
+
+    lax.fori_loop(0, SLOTS // 64, start_load, 0)
     flat_to_by_vector(block_x, temp, vec_x)
     own[0] = vec_x[...].astype(BF16)
     norm = lax.dot_general(vec_x[...], vec_x[...], NT, precision=HIGHEST, preferred_element_type=F32)
     gram_own[0] = jnp.zeros((K, 128), F32)
     gram_own[0, :, 0:K] = norm
-
-    pl.semaphore_wait(barrier, N_ROW + N_COL - 2)
-
-    def gather(step):
-        source = lambda peer: own.at[step]
-        send_all("row", step, source, got_r.at[step])
-        send_all("col", step, source, got_c.at[step])
-
-    def gram_row(which):
-        source = lambda peer: gram_own.at[which]
-        send_all("row", 4 + which, source, gram_r.at[which])
-        gram_r[which, my_row] = gram_own[which]
-
-    def gram_col(which):
-        each_arrival("row", 4 + which, lambda s: gram_own.at[which], gram_r.at[which], lambda s, c: c)
-        gram_own[3 + which] = jnp.sum(gram_r[which], axis=0)
-        source = lambda peer: gram_own.at[3 + which]
-        send_all("col", 4 + which, source, gram_c.at[which])
-        gram_c[which, my_col] = gram_own[3 + which]
-
-    def gram_done(which):
-        each_arrival("col", 4 + which, lambda s: gram_own.at[3 + which], gram_c.at[which], lambda s, c: c)
-        return jnp.sum(gram_c[which], axis=0)[:, 0:K]
-
-    gather(0)
-    gram_row(0)
-
     count = count_s[0, 0]
 
     def arrange(chunk, carry):
@@ -319,7 +286,45 @@
         load_groups(raw, stage, tiles, chunk, count)
         return carry
 
-    lax.fori_loop(0, SLOTS // 64, arrange, 0)
+    lax.fori_loop(0, EARLY_CHUNKS, arrange, 0)
+    pl.semaphore_wait(barrier, N_ROW + N_COL - 2)
+
+    def gather(step):
+        send_all("row", step, lambda peer: own.at[step], got_r.at[step])
+        send_all("col", step, lambda peer: own.at[step], got_c.at[step])
+
+    def gram_row(which):
+        send_all("row", 4 + which, lambda peer: gram_own.at[which], gram_r.at[which])
+        gram_r[which, my_row] = gram_own[which]
+
+    def gram_col(which):
+        wait_bytes(gram_r.at[which], "row", gram_recv_r.at[which])
+        gram_own[3 + which] = jnp.sum(gram_r[which], axis=0)
+        send_all("col", 4 + which, lambda peer: gram_own.at[3 + which], gram_c.at[which])
+        gram_c[which, my_col] = gram_own[3 + which]
+
+    def gram_done(which):
+        wait_bytes(gram_c.at[which], "col", gram_recv_c.at[which])
+        return jnp.sum(gram_c[which], axis=0)[:, 0:K]
+
+    def cross_part(step):
+        def dot(slot, carry):
+            return carry + lax.dot_general(part_c[step, slot], got_c[step, slot], NT, preferred_element_type=F32)
+
+        return lax.fori_loop(0, N_COL, dot, jnp.zeros((K, K), F32), unroll=True)
+
+    def finish_sends(step):
+        wait_bytes(got_r.at[step], "row", send_r.at[step])
+        wait_bytes(got_c.at[step], "col", send_c.at[step])
+        wait_bytes(part_r.at[step], "row", send_r.at[2 + step])
+        wait_bytes(part_c.at[step], "col", send_c.at[2 + step])
+        for which in (0, 1) if step == 0 else (2,):
+            wait_bytes(gram_r.at[which], "row", send_r.at[4 + which])
+            wait_bytes(gram_c.at[which], "col", send_c.at[4 + which])
+
+    gather(0)
+    gram_row(0)
+    lax.fori_loop(EARLY_CHUNKS, SLOTS // 64, arrange, 0)
     for s in range(2):
         columns = jnp.concatenate(
             [col_v[0, :, s * 256 : s * 256 + 256], col_v[0, :, 512 + s * 256 : 768 + s * 256]], axis=1
@@ -331,8 +336,6 @@
     gram_col(0)
 
     def product(step, while_waiting):
-        source = lambda s: own.at[step]
-
         def enter(buffer, table):
             def use(slot, carry):
                 fill_table(buffer.at[step, slot], table, slot * SEGB)
@@ -341,74 +344,71 @@
             return use
 
         fill_table(own.at[step], table_r, my_row * SEGB)
-        each_arrival("row", step, source, got_r.at[step], enter(got_r, table_r))
+        each_arrival("row", step, got_r.at[step], enter(got_r, table_r))
         multiply(row_s, table_r, tiles, prod_c, False, turned if step == 0 else None)
-        add_up(place_c, prod_c, part_c.at[step], CB)
+        add_up(place_c, prod_c, temp, part_c.at[step], CB)
         send_all("col", 2 + step, lambda peer: part_c.at[step, peer], sum_c.at[step])
         fill_table(own.at[step], table_c, my_col * SEGB)
-        each_arrival("col", step, source, got_c.at[step], enter(got_c, table_c))
+        got_c[step, my_col] = own[step]
+        each_arrival("col", step, got_c.at[step], enter(got_c, table_c))
+        gram_own[1 + step] = jnp.zeros((K, 128), F32)
+        gram_own[1 + step, :, 0:K] = cross_part(step)
+        gram_row(1 + step)
         multiply(col_s, table_c, turned, prod_r, True)
-        add_up(place_r, prod_r, part_r.at[step], RB)
+        add_up(place_r, prod_r, temp, part_r.at[step], RB)
         send_all("row", 2 + step, lambda peer: part_r.at[step, peer], sum_r.at[step])
+        gram_col(1 + step)
         extra = while_waiting()
-        total = part_c[step, my_col].astype(F32) + part_r[step, my_row].astype(F32)
+        vec_a[...] = part_c[step, my_col].astype(F32) + part_r[step, my_row].astype(F32)
 
         def add(buffer):
-            return lambda slot, carry: carry + buffer[step, slot].astype(F32)
-
-        total = each_arrival("col", 2 + step, lambda s: part_c.at[step, s], sum_c.at[step], add(sum_c), total)
-        total = each_arrival("row", 2 + step, lambda s: part_r.at[step, s], sum_r.at[step], add(sum_r), total)
-        by_row[...] = total
-        return extra
-
-    inverse, scale = product(0, lambda: factor(gram_done(0)))
-    by_row_to_by_vector(by_row, temp, vec_a)
-    gram_own[1] = jnp.zeros((K, 128), F32)
-    gram_own[1, :, 0:K] = lax.dot_general(vec_a[...], vec_x[...], NT, precision=HIGHEST, preferred_element_type=F32)
-    gram_row(1)
-    gram_col(1)
-    cross = gram_done(1)
+            def use(slot, carry):
+                vec_a[...] += buffer[step, slot].astype(F32)
+                return carry
+
+            return use
+
+        each_arrival("col", 2 + step, sum_c.at[step], add(sum_c))
+        each_arrival("row", 2 + step, sum_r.at[step], add(sum_r))
+        half = gram_done(1 + step)
+        return half + half.T, extra
+
+    cross, (inverse, scale) = product(0, lambda: factor(gram_done(0)))
     halfway = lax.dot_general(inverse, cross, NT, precision=HIGHEST, preferred_element_type=F32) * scale
     coupling = lax.dot_general(
         halfway, inverse, (((0,), (0,)), ((), ())), precision=HIGHEST, preferred_element_type=F32
     )
-    vec_a[...] = vec_a[...] - jnp.dot(coupling, vec_x[...], precision=HIGHEST, preferred_element_type=F32)
-    own[1] = vec_a[...].astype(BF16)
+    residual = vec_a[...] - jnp.dot(coupling, vec_x[...], precision=HIGHEST, preferred_element_type=F32)
+    own[1] = residual.astype(BF16)
     gather(1)
-    by_vector_to_by_row(vec_a, temp, by_row)
-    by_row_to_flat(by_row, residual_out)
-
-    product(1, lambda: None)
-    by_row_to_by_vector(by_row, temp, vec_b)
-    gram_own[2] = jnp.zeros((K, 128), F32)
-    gram_own[2, :, 0:K] = lax.dot_general(vec_a[...], vec_b[...], NT, precision=HIGHEST, preferred_element_type=F32)
-    gram_row(2)
-    by_row_to_flat(by_row, image_out)
-    gram_col(2)
-    gram_out[...] = gram_done(2) * (1.0 / (N_ROW * N_COL * SEGB * TILE))
-
-    for step in range(2):
-        source = lambda peer, step=step: own.at[step]
-        finish_sends("row", step, source, got_r.at[step])
-        finish_sends("col", step, source, got_c.at[step])
-        finish_sends("row", 2 + step, lambda peer, step=step: part_r.at[step, peer], sum_r.at[step])
-        finish_sends("col", 2 + step, lambda peer, step=step: part_c.at[step, peer], sum_c.at[step])
-    for which in range(3):
-        finish_sends("row", 4 + which, lambda peer, which=which: gram_own.at[which], gram_r.at[which])
-        finish_sends("col", 4 + which, lambda peer, which=which: gram_own.at[3 + which], gram_c.at[which])
+    residual_out[...] = residual
+    finish_sends(0)
+
+    last, _ = product(1, lambda: None)
+    image_out[...] = vec_a[...]
+    gram_out[...] = last * (1.0 / (N_ROW * N_COL * SEGB * TILE))
+    finish_sends(1)
+
+
+def lay_flat(residual, image, gram, residual_out, image_out, gram_out, temp, by_row):
+    for source, target in ((residual, residual_out), (image, image_out)):
+        by_vector_to_by_row(source, temp, by_row)
+        by_row_to_flat(by_row, target)
+    gram_out[...] = gram[...]
 
 
 def local(block_x, tile_values, row_block, col_block, tile_counts):
     vmem = pl.BlockSpec(memory_space=pltpu.VMEM)
     smem = pl.BlockSpec(memory_space=pltpu.SMEM)
     kinds = 7
-    return pl.pallas_call(
+    vectors = (
+        jax.ShapeDtypeStruct((SEGB, WIDTH), F32),
+        jax.ShapeDtypeStruct((SEGB, WIDTH), F32),
+        jax.ShapeDtypeStruct((K, K), F32),
+    )
+    results = pl.pallas_call(
         kernel,
-        out_shape=(
-            jax.ShapeDtypeStruct((SEGB, WIDTH), F32),
-            jax.ShapeDtypeStruct((SEGB, WIDTH), F32),
-            jax.ShapeDtypeStruct((K, K), F32),
-        ),
+        out_shape=vectors,
         in_specs=[vmem, pl.BlockSpec(memory_space=pl.ANY), smem, smem, smem, vmem, vmem],
         out_specs=(vmem, vmem, vmem),
         scratch_shapes=[
@@ -422,32 +422,39 @@
             pltpu.VMEM((2 * CB, 512), BF16),
             pltpu.VMEM((K * Y_PITCH, 128), F32),
             pltpu.VMEM((K * Y_PITCH, 128), F32),
-            pltpu.VMEM((128, 128), F32),
-            pltpu.VMEM((128, 128), F32),
-            pltpu.VMEM((K, WIDTH), F32),
+            pltpu.VMEM((N_COL * 128, 128), F32),
             pltpu.VMEM((K, WIDTH), F32),
             pltpu.VMEM((K, WIDTH), F32),
             pltpu.VMEM((2, K, WIDTH), BF16),
             pltpu.VMEM((2, N_ROW, K, WIDTH), BF16),
             pltpu.VMEM((2, N_COL, K, WIDTH), BF16),
-            pltpu.VMEM((2, N_ROW, 128, 128), BF16),
-            pltpu.VMEM((2, N_COL, 128, 128), BF16),
-            pltpu.VMEM((2, N_ROW, 128, 128), BF16),
-            pltpu.VMEM((2, N_COL, 128, 128), BF16),
+            pltpu.VMEM((2, N_ROW, K, WIDTH), BF16),
+            pltpu.VMEM((2, N_COL, K, WIDTH), BF16),
+            pltpu.VMEM((2, N_ROW, K, WIDTH), BF16),
+            pltpu.VMEM((2, N_COL, K, WIDTH), BF16),
             pltpu.VMEM((6, K, 128), F32),
             pltpu.VMEM((3, N_ROW, K, 128), F32),
             pltpu.VMEM((3, N_COL, K, 128), F32),
             pltpu.SemaphoreType.DMA((SLOTS // 64, 4)),
-            pltpu.SemaphoreType.DMA((kinds, N_ROW)),
-            pltpu.SemaphoreType.DMA((kinds, N_COL)),
-            pltpu.SemaphoreType.DMA((kinds, N_ROW)),
-            pltpu.SemaphoreType.DMA((kinds, N_COL)),
+            pltpu.SemaphoreType.DMA((kinds,)),
+            pltpu.SemaphoreType.DMA((kinds,)),
+            pltpu.SemaphoreType.DMA((4, N_ROW)),
+            pltpu.SemaphoreType.DMA((4, N_COL)),
+            pltpu.SemaphoreType.DMA((3,)),
+            pltpu.SemaphoreType.DMA((3,)),
         ],
         compiler_params=pltpu.CompilerParams(
             collective_id=0, has_side_effects=True, vmem_limit_bytes=58 << 20
         ),
         cost_estimate=pl.CostEstimate(flops=1 << 30, bytes_accessed=9 << 20, transcendentals=0),
     )(block_x, tile_values, row_block, col_block, tile_counts, row_block, col_block)
+    return pl.pallas_call(
+        lay_flat,
+        out_shape=vectors,
+        in_specs=[vmem] * 3,
+        out_specs=(vmem, vmem, vmem),
+        scratch_shapes=[pltpu.VMEM((128, 128), F32), pltpu.VMEM((128, 128), F32)],
+    )(*results)
 
 
 def solution(mesh):

time: 89.1 us -> 73.3 us (0.82)
  Pallas kernels: 83.2 us -> 71.8 us
  local copies, waits for them, and re-layouts: 4.24 us -> 0 us
    pallas_call x1 -> x2, Pallas kernels: 83.2 us -> 71.8 us  [the longest x1 70.1 us: local(): pl.pallas_call(kernel, out_shape=vectors, in_specs=[vmem, pl.BlockSpec(me...]
    unnamed x3 -> x0, local copies, waits for them, and re-layouts: 4.24 us -> none
where the time goes in v2:
time: 73.3 us; the launch traced here: 73.1 us
  Pallas kernels  71.8 us (98%)
  between operations  1.29 us (2%)
    pallas_call x1, Pallas kernels, local(): pl.pallas_call(kernel, out_shape=vectors, in_specs=[vmem, pl.BlockSpec(me...  70.1 us
    pallas_call x1, Pallas kernels, local(): pl.pallas_call(lay_flat, out_shape=vectors, in_specs=[vmem] * 3, out_spec...  1.65 us

profile of v2, /device:TPU:1, one launch (start us, length us, event | category | flops | bytes accessed | tf_op | source)
XLA Modules:
  0.0 73.1 jit_solution(15814089887726875656)
XLA Ops:
  1.3 70.1 %shard_map.76 = (f32[16,1024]{1,0:T(8,128)}, f32[16,1024]{1,0:T(8,128)}, f32[16,16]{1,0:T(8,128)}) custom-call(f32[16,1024]{1,0:T(8,128)} %block_x.1, bf16[1,1,1024,4096]{3,2,1,0:T(8,128)(2,1)} %tile_values.1, s32[1,1,1024]{2,1,0:T(1,128)} %row_v.1, s32[1,1,1024]{2,1,0:T(1,128)} %col_v.1, s32[1,1]{1,0:T(1,128)S(6)} %copy.8.count_s, s32[1,1,1024]{2,1,0:T(1,128)} %row_v.1, ...), custom_call_target="tpu_custom_call" | custom-call | flops 1073741824 | bytes 9437184 | tf_op jit(solution)/shard_map/pallas_call | solution.py:409
  71.4 1.7 %shard_map.77 = (f32[16,1024]{1,0:T(8,128)}, f32[16,1024]{1,0:T(8,128)}, f32[16,16]{1,0:T(8,128)}) custom-call(f32[16,1024]{1,0:T(8,128)} %get-tuple-element.6.residual, f32[16,1024]{1,0:T(8,128)} %get-tuple-element.7.image, f32[16,16]{1,0:T(8,128)} %get-tuple-element.8.gram), custom_call_target="tpu_custom_call" | custom-call | tf_op jit(solution)/shard_map/pallas_call | solution.py:451

commit v3 on v2

--- a/solution.py
+++ b/solution.py
@@ -17,6 +17,7 @@
 WIDTH = K * TILE
 N_ROW = 8
 N_COL = 16
+N_CHIP = N_COL // 2
 RB = N_ROW * SEGB
 CB = N_COL * SEGB
 STAGE_PITCH = 136
@@ -156,7 +157,7 @@
     lax.fori_loop(0, GROUPS, step, 0, unroll=64)
 
 
-def add_up(places, products, temp, out, blocks):
+def add_up(places, products, temp, blocks):
     lt = left_half(8)
     targets = blocks // SEGB
 
@@ -179,13 +180,27 @@
 
     lax.fori_loop(0, K // 2, step, 0, unroll=True)
 
-    def narrow(target, carry):
+
+def narrow_sums(temp, first, stride, out, count):
+    def step(target, carry):
         for p in range(8):
-            rows = pl.ds(pl.multiple_of(target * 128 + p * K, K), K)
-            out[target, :, p * 128 : p * 128 + 128] = temp[rows, :].astype(BF16)
-        return carry
-
-    lax.fori_loop(0, targets, narrow, 0, unroll=True)
+            start = (first + target * stride) * 128 + p * K
+            out[target, :, p * 128 : p * 128 + 128] = temp[pl.ds(pl.multiple_of(start, K), K), :].astype(BF16)
+        return carry
+
+    lax.fori_loop(0, count, step, 0, unroll=True)
+
+
+def add_pair(temp, first, other, out, count):
+    def step(target, carry):
+        for p in range(8):
+            start = (first + target * 2) * 128 + p * K
+            here = temp[pl.ds(pl.multiple_of(start, K), K), :]
+            lanes = slice(p * 128, p * 128 + 128)
+            out[target, :, lanes] = (here + other[target, :, lanes].astype(F32)).astype(BF16)
+        return carry
+
+    lax.fori_loop(0, count, step, 0, unroll=True)
 
 
 def factor(norm):
@@ -211,43 +226,28 @@
     block_x, tile_values, row_s, col_s, count_s, row_v, col_v,
     residual_out, image_out, gram_out,
     raw, stage, tiles, turned, table_r, table_c, place_r, place_c, prod_r, prod_c,
-    temp, vec_x, vec_a, own, got_r, got_c, part_r, part_c, sum_r, sum_c, gram_own, gram_r, gram_c,
-    load_sem, send_r, send_c, recv_r, recv_c, gram_recv_r, gram_recv_c,
+    temp, vec_x, vec_a, own, got_r, got_c, part_r, part_c, pair_c, both_c, sum_r, sum_c, gram_own, gram_r, gram_c,
+    load_sem, send_r, send_c, recv_r, recv_c, recv_sum_r, recv_sum_c, pair_sem, gram_recv_r, gram_recv_c,
 ):
     my_row, my_col = lax.axis_index("row"), lax.axis_index("col")
-    size_of = {"row": N_ROW, "col": N_COL}
-    me_of = {"row": my_row, "col": my_col}
-    send_of = {"row": send_r, "col": send_c}
-    recv_of = {"row": recv_r, "col": recv_c}
-    gram_recv_of = {"row": gram_recv_r, "col": gram_recv_c}
-
-    def send_all(axis, kind, source_of, buffer):
-        size, me = size_of[axis], me_of[axis]
-        arrived = recv_of[axis].at[kind, me] if kind < 4 else gram_recv_of[axis].at[kind - 4]
-
+    my_chip, my_core = my_col // 2, lax.rem(my_col, 2)
+    sibling = my_chip * 2 + 1 - my_core
+
+    def send(axis, peer, source, target, sent, arrived):
+        pltpu.make_async_remote_copy(
+            src_ref=source, dst_ref=target, send_sem=sent, recv_sem=arrived,
+            device_id={axis: peer}, device_id_type=pl.DeviceIdType.MESH,
+        ).start()
+
+    def others(size, me, use):
         def step(d, carry):
-            peer = lax.rem(me + d, size)
-            pltpu.make_async_remote_copy(
-                src_ref=source_of(peer), dst_ref=buffer.at[me], send_sem=send_of[axis].at[kind], recv_sem=arrived,
-                device_id={axis: peer}, device_id_type=pl.DeviceIdType.MESH,
-            ).start()
+            use(lax.rem(me + d, size))
             return carry
 
         lax.fori_loop(1, size, step, 0)
 
-    def wait_bytes(buffer, axis, sem):
-        block = buffer.at[pl.ds(0, size_of[axis] - 1)]
+    def wait_bytes(block, sem):
         pltpu.make_async_copy(block, block, sem).wait()
-
-    def each_arrival(axis, kind, buffer, use, start=0):
-        size, me = size_of[axis], me_of[axis]
-
-        def step(d, carry):
-            slot = lax.rem(me + size - d, size)
-            pltpu.make_async_copy(buffer.at[slot], buffer.at[slot], recv_of[axis].at[kind, slot]).wait()
-            return use(slot, carry)
-
-        return lax.fori_loop(1, size, step, start)
 
     def load(chunk, g):
         return pltpu.make_async_copy(
@@ -261,23 +261,23 @@
         return carry
 
     barrier = pltpu.get_barrier_semaphore()
-    for axis in ("row", "col"):
-
-        def greet(d, carry, axis=axis):
-            pl.semaphore_signal(
-                barrier, inc=1, device_id={axis: lax.rem(me_of[axis] + d, size_of[axis])},
-                device_id_type=pl.DeviceIdType.MESH,
-            )
-            return carry
-
-        lax.fori_loop(1, size_of[axis], greet, 0)
+
+    def greet(axis, peer):
+        pl.semaphore_signal(barrier, inc=1, device_id={axis: peer}, device_id_type=pl.DeviceIdType.MESH)
+
+    others(N_ROW, my_row, lambda peer: greet("row", peer))
+    others(N_COL, my_col, lambda peer: greet("col", peer))
+
+    def put_gram(which, value):
+        gram_own[which] = jnp.zeros((8, 128), F32)
+        gram_own[which, :, 0:K] = value[0:8]
+        gram_own[which, :, K : 2 * K] = value[8:16]
 
     lax.fori_loop(0, SLOTS // 64, start_load, 0)
     flat_to_by_vector(block_x, temp, vec_x)
     own[0] = vec_x[...].astype(BF16)
     norm = lax.dot_general(vec_x[...], vec_x[...], NT, precision=HIGHEST, preferred_element_type=F32)
-    gram_own[0] = jnp.zeros((K, 128), F32)
-    gram_own[0, :, 0:K] = norm
+    put_gram(0, norm)
     count = count_s[0, 0]
 
     def arrange(chunk, carry):
@@ -290,37 +290,69 @@
     pl.semaphore_wait(barrier, N_ROW + N_COL - 2)
 
     def gather(step):
-        send_all("row", step, lambda peer: own.at[step], got_r.at[step])
-        send_all("col", step, lambda peer: own.at[step], got_c.at[step])
+        def to_row(peer):
+            send("row", peer, own.at[step], got_r.at[step, my_row], send_r.at[step], recv_r.at[step, my_row])
+
+        def to_col(peer):
+            send("col", peer, own.at[step], got_c.at[step, my_col], send_c.at[step], recv_c.at[step, my_col])
+
+        others(N_ROW, my_row, to_row)
+        others(N_CHIP, my_chip, lambda chip: to_col(chip * 2 + my_core))
+        to_col(sibling)
+        got_c[step, my_col] = own[step]
+
+    def forward(step):
+        def pass_on(chip):
+            slot = chip * 2 + my_core
+            wait_bytes(got_c.at[step, slot], recv_c.at[step, slot])
+            send(
+                "col", sibling, got_c.at[step, slot], got_c.at[step, slot], send_c.at[step], recv_c.at[step, slot]
+            )
+
+        others(N_CHIP, my_chip, pass_on)
 
     def gram_row(which):
-        send_all("row", 4 + which, lambda peer: gram_own.at[which], gram_r.at[which])
+        def to_row(peer):
+            send(
+                "row", peer, gram_own.at[which], gram_r.at[which, my_row], send_r.at[4 + which], gram_recv_r.at[which]
+            )
+
+        others(N_ROW, my_row, to_row)
         gram_r[which, my_row] = gram_own[which]
 
     def gram_col(which):
-        wait_bytes(gram_r.at[which], "row", gram_recv_r.at[which])
+        wait_bytes(gram_r.at[which, pl.ds(0, N_ROW - 1)], gram_recv_r.at[which])
         gram_own[3 + which] = jnp.sum(gram_r[which], axis=0)
-        send_all("col", 4 + which, lambda peer: gram_own.at[3 + which], gram_c.at[which])
+
+        def to_col(peer):
+            send(
+                "col", peer, gram_own.at[3 + which], gram_c.at[which, my_col], send_c.at[4 + which],
+                gram_recv_c.at[which],
+            )
+
+        others(N_COL, my_col, to_col)
         gram_c[which, my_col] = gram_own[3 + which]
 
     def gram_done(which):
-        wait_bytes(gram_c.at[which], "col", gram_recv_c.at[which])
-        return jnp.sum(gram_c[which], axis=0)[:, 0:K]
+        wait_bytes(gram_c.at[which, pl.ds(0, N_COL - 1)], gram_recv_c.at[which])
+        total = jnp.sum(gram_c[which], axis=0)
+        return jnp.concatenate([total[:, 0:K], total[:, K : 2 * K]], axis=0)
 
     def cross_part(step):
-        def dot(slot, carry):
-            return carry + lax.dot_general(part_c[step, slot], got_c[step, slot], NT, preferred_element_type=F32)
-
-        return lax.fori_loop(0, N_COL, dot, jnp.zeros((K, K), F32), unroll=True)
+        def dot(chip, carry):
+            slot = chip * 2 + my_core
+            return carry + lax.dot_general(both_c[step, chip], got_c[step, slot], NT, preferred_element_type=F32)
+
+        return lax.fori_loop(0, N_CHIP, dot, jnp.zeros((K, K), F32), unroll=True)
 
     def finish_sends(step):
-        wait_bytes(got_r.at[step], "row", send_r.at[step])
-        wait_bytes(got_c.at[step], "col", send_c.at[step])
-        wait_bytes(part_r.at[step], "row", send_r.at[2 + step])
-        wait_bytes(part_c.at[step], "col", send_c.at[2 + step])
+        wait_bytes(got_r.at[step, pl.ds(0, N_ROW - 1)], send_r.at[step])
+        wait_bytes(got_c.at[step, pl.ds(0, N_COL - 1)], send_c.at[step])
+        wait_bytes(got_r.at[step, pl.ds(0, N_ROW - 1)], send_r.at[2 + step])
+        wait_bytes(got_c.at[step, pl.ds(0, N_COL - 1)], send_c.at[2 + step])
         for which in (0, 1) if step == 0 else (2,):
-            wait_bytes(gram_r.at[which], "row", send_r.at[4 + which])
-            wait_bytes(gram_c.at[which], "col", send_c.at[4 + which])
+            wait_bytes(gram_r.at[which, pl.ds(0, N_ROW - 1)], send_r.at[4 + which])
+            wait_bytes(gram_c.at[which, pl.ds(0, N_COL - 1)], send_c.at[4 + which])
 
     gather(0)
     gram_row(0)
@@ -336,40 +368,67 @@
     gram_col(0)
 
     def product(step, while_waiting):
-        def enter(buffer, table):
-            def use(slot, carry):
-                fill_table(buffer.at[step, slot], table, slot * SEGB)
-                return carry
-
-            return use
+        def enter_row(peer):
+            wait_bytes(got_r.at[step, peer], recv_r.at[step, peer])
+            fill_table(got_r.at[step, peer], table_r, peer * SEGB)
+
+        def enter_same(chip):
+            slot = chip * 2 + my_core
+            fill_table(got_c.at[step, slot], table_c, slot * SEGB)
+
+        def enter_other(chip):
+            slot = chip * 2 + 1 - my_core
+            wait_bytes(got_c.at[step, slot], recv_c.at[step, slot])
+            fill_table(got_c.at[step, slot], table_c, slot * SEGB)
 
         fill_table(own.at[step], table_r, my_row * SEGB)
-        each_arrival("row", step, got_r.at[step], enter(got_r, table_r))
+        others(N_ROW, my_row, enter_row)
         multiply(row_s, table_r, tiles, prod_c, False, turned if step == 0 else None)
-        add_up(place_c, prod_c, temp, part_c.at[step], CB)
-        send_all("col", 2 + step, lambda peer: part_c.at[step, peer], sum_c.at[step])
-        fill_table(own.at[step], table_c, my_col * SEGB)
-        got_c[step, my_col] = own[step]
-        each_arrival("col", step, got_c.at[step], enter(got_c, table_c))
-        gram_own[1 + step] = jnp.zeros((K, 128), F32)
-        gram_own[1 + step, :, 0:K] = cross_part(step)
+        forward(step)
+        add_up(place_c, prod_c, temp, CB)
+        narrow_sums(temp, 1 - my_core, 2, part_c.at[step], N_CHIP)
+        send("col", sibling, part_c.at[step], pair_c.at[step], send_c.at[2 + step], pair_sem.at[step])
+        enter_same(my_chip)
+        others(N_CHIP, my_chip, enter_same)
+        enter_other(my_chip)
+        others(N_CHIP, my_chip, enter_other)
+        wait_bytes(pair_c.at[step], pair_sem.at[step])
+        add_pair(temp, my_core, pair_c.at[step], both_c.at[step], N_CHIP)
+        put_gram(1 + step, cross_part(step))
         gram_row(1 + step)
+
+        def sums_to_col(chip):
+            send(
+                "col", chip * 2 + my_core, both_c.at[step, chip], sum_c.at[step, my_chip], send_c.at[2 + step],
+                recv_sum_c.at[step, my_chip],
+            )
+
+        others(N_CHIP, my_chip, sums_to_col)
         multiply(col_s, table_c, turned, prod_r, True)
-        add_up(place_r, prod_r, temp, part_r.at[step], RB)
-        send_all("row", 2 + step, lambda peer: part_r.at[step, peer], sum_r.at[step])
+        add_up(place_r, prod_r, temp, RB)
+        narrow_sums(temp, 0, 1, part_r.at[step], N_ROW)
         gram_col(1 + step)
+
+        def sums_to_row(peer):
+            send(
+                "row", peer, part_r.at[step, peer], sum_r.at[step, my_row], send_r.at[2 + step],
+                recv_sum_r.at[step, my_row],
+            )
+
+        others(N_ROW, my_row, sums_to_row)
         extra = while_waiting()
-        vec_a[...] = part_c[step, my_col].astype(F32) + part_r[step, my_row].astype(F32)
-
-        def add(buffer):
-            def use(slot, carry):
-                vec_a[...] += buffer[step, slot].astype(F32)
-                return carry
-
-            return use
-
-        each_arrival("col", 2 + step, sum_c.at[step], add(sum_c))
-        each_arrival("row", 2 + step, sum_r.at[step], add(sum_r))
+        vec_a[...] = both_c[step, my_chip].astype(F32) + part_r[step, my_row].astype(F32)
+
+        def add_col(chip):
+            wait_bytes(sum_c.at[step, chip], recv_sum_c.at[step, chip])
+            vec_a[...] += sum_c[step, chip].astype(F32)
+
+        def add_row(peer):
+            wait_bytes(sum_r.at[step, peer], recv_sum_r.at[step, peer])
+            vec_a[...] += sum_r[step, peer].astype(F32)
+
+        others(N_CHIP, my_chip, add_col)
+        others(N_ROW, my_row, add_row)
         half = gram_done(1 + step)
         return half + half.T, extra
 
@@ -429,17 +488,22 @@
             pltpu.VMEM((2, N_ROW, K, WIDTH), BF16),
             pltpu.VMEM((2, N_COL, K, WIDTH), BF16),
             pltpu.VMEM((2, N_ROW, K, WIDTH), BF16),
-            pltpu.VMEM((2, N_COL, K, WIDTH), BF16),
+            pltpu.VMEM((2, N_CHIP, K, WIDTH), BF16),
+            pltpu.VMEM((2, N_CHIP, K, WIDTH), BF16),
+            pltpu.VMEM((2, N_CHIP, K, WIDTH), BF16),
             pltpu.VMEM((2, N_ROW, K, WIDTH), BF16),
-            pltpu.VMEM((2, N_COL, K, WIDTH), BF16),
-            pltpu.VMEM((6, K, 128), F32),
-            pltpu.VMEM((3, N_ROW, K, 128), F32),
-            pltpu.VMEM((3, N_COL, K, 128), F32),
+            pltpu.VMEM((2, N_CHIP, K, WIDTH), BF16),
+            pltpu.VMEM((6, 8, 128), F32),
+            pltpu.VMEM((3, N_ROW, 8, 128), F32),
+            pltpu.VMEM((3, N_COL, 8, 128), F32),
             pltpu.SemaphoreType.DMA((SLOTS // 64, 4)),
             pltpu.SemaphoreType.DMA((kinds,)),
             pltpu.SemaphoreType.DMA((kinds,)),
-            pltpu.SemaphoreType.DMA((4, N_ROW)),
-            pltpu.SemaphoreType.DMA((4, N_COL)),
+            pltpu.SemaphoreType.DMA((2, N_ROW)),
+            pltpu.SemaphoreType.DMA((2, N_COL)),
+            pltpu.SemaphoreType.DMA((2, N_ROW)),
+            pltpu.SemaphoreType.DMA((2, N_CHIP)),
+            pltpu.SemaphoreType.DMA((2,)),
             pltpu.SemaphoreType.DMA((3,)),
             pltpu.SemaphoreType.DMA((3,)),
         ],

time: 73.3 us -> 63 us (0.86)
  Pallas kernels: 71.8 us -> 61.5 us
    pallas_call x1, Pallas kernels: 70.1 us -> 59.8 us  [local(): pl.pallas_call(kernel, out_shape=vectors, in_specs=[vmem, pl.BlockSpec(me...]
where the time goes in v3:
time: 63 us; the launch traced here: 62.8 us
  Pallas kernels  61.5 us (98%)
  between operations  1.29 us (2%)
    pallas_call x1, Pallas kernels, local(): pl.pallas_call(kernel, out_shape=vectors, in_specs=[vmem, pl.BlockSpec(me...  59.8 us
    pallas_call x1, Pallas kernels, local(): pl.pallas_call(lay_flat, out_shape=vectors, in_specs=[vmem] * 3, out_spec...  1.65 us

profile of v3, /device:TPU:1, one launch (start us, length us, event | category | flops | bytes accessed | tf_op | source)
XLA Modules:
  0.0 62.8 jit_solution(13064703797844666774)
XLA Ops:
  1.3 59.8 %shard_map.76 = (f32[16,1024]{1,0:T(8,128)}, f32[16,1024]{1,0:T(8,128)}, f32[16,16]{1,0:T(8,128)}) custom-call(f32[16,1024]{1,0:T(8,128)} %block_x.1, bf16[1,1,1024,4096]{3,2,1,0:T(8,128)(2,1)} %tile_values.1, s32[1,1,1024]{2,1,0:T(1,128)} %row_v.1, s32[1,1,1024]{2,1,0:T(1,128)} %col_v.1, s32[1,1]{1,0:T(1,128)S(6)} %copy.8.count_s, s32[1,1,1024]{2,1,0:T(1,128)} %row_v.1, ...), custom_call_target="tpu_custom_call" | custom-call | flops 1073741824 | bytes 9437184 | tf_op jit(solution)/shard_map/pallas_call | solution.py:468
  61.1 1.7 %shard_map.77 = (f32[16,1024]{1,0:T(8,128)}, f32[16,1024]{1,0:T(8,128)}, f32[16,16]{1,0:T(8,128)}) custom-call(f32[16,1024]{1,0:T(8,128)} %get-tuple-element.6.residual, f32[16,1024]{1,0:T(8,128)} %get-tuple-element.7.image, f32[16,16]{1,0:T(8,128)} %get-tuple-element.8.gram), custom_call_target="tpu_custom_call" | custom-call | tf_op jit(solution)/shard_map/pallas_call | solution.py:515

commit v4 on v3

--- a/solution.py
+++ b/solution.py
@@ -154,7 +154,7 @@
             products[pl.ds(8 * Y_PITCH + place, 8, stride=Y_PITCH), :] = merged[8:]
         return carry
 
-    lax.fori_loop(0, GROUPS, step, 0, unroll=64)
+    lax.fori_loop(0, GROUPS, step, 0, unroll=128)
 
 
 def add_up(places, products, temp, blocks):
@@ -223,11 +223,11 @@
 
 
 def kernel(
-    block_x, tile_values, row_s, col_s, count_s, row_v, col_v,
+    block_x, tile_values, row_block, col_block, tile_counts,
     residual_out, image_out, gram_out,
     raw, stage, tiles, turned, table_r, table_c, place_r, place_c, prod_r, prod_c,
-    temp, vec_x, vec_a, own, got_r, got_c, part_r, part_c, pair_c, both_c, sum_r, sum_c, gram_own, gram_r, gram_c,
-    load_sem, send_r, send_c, recv_r, recv_c, recv_sum_r, recv_sum_c, pair_sem, gram_recv_r, gram_recv_c,
+    flat_x, row_s, col_s, count_s, row_v, col_v, temp, by_row, vec_x, vec_a, vec_b, gram_last, own, got_r, got_c, part_r, part_c, pair_c, both_c, spare, sum_r, sum_c, gram_own, gram_r, gram_c,
+    enter_sem, leave_sem, load_sem, send_r, send_c, recv_r, recv_c, recv_sum_r, recv_sum_c, pair_sem, gram_recv_r, gram_recv_c,
 ):
     my_row, my_col = lax.axis_index("row"), lax.axis_index("col")
     my_chip, my_core = my_col // 2, lax.rem(my_col, 2)
@@ -273,11 +273,24 @@
         gram_own[which, :, 0:K] = value[0:8]
         gram_own[which, :, K : 2 * K] = value[8:16]
 
+    pairs = (
+        (block_x, flat_x), (tile_counts, count_s), (row_block, row_s), (col_block, col_s),
+        (row_block, row_v), (col_block, col_v),
+    )
+    enter = [pltpu.make_async_copy(a, b, enter_sem.at[i]) for i, (a, b) in enumerate(pairs)]
+
+    def leave(which, source, target):
+        return pltpu.make_async_copy(source, target, leave_sem.at[which])
+
+    for arrival in enter:
+        arrival.start()
     lax.fori_loop(0, SLOTS // 64, start_load, 0)
-    flat_to_by_vector(block_x, temp, vec_x)
+    enter[0].wait()
+    flat_to_by_vector(flat_x, temp, vec_x)
     own[0] = vec_x[...].astype(BF16)
     norm = lax.dot_general(vec_x[...], vec_x[...], NT, precision=HIGHEST, preferred_element_type=F32)
     put_gram(0, norm)
+    enter[1].wait()
     count = count_s[0, 0]
 
     def arrange(chunk, carry):
@@ -289,25 +302,27 @@
     lax.fori_loop(0, EARLY_CHUNKS, arrange, 0)
     pl.semaphore_wait(barrier, N_ROW + N_COL - 2)
 
-    def gather(step):
+    def gather(step, beside):
         def to_row(peer):
             send("row", peer, own.at[step], got_r.at[step, my_row], send_r.at[step], recv_r.at[step, my_row])
 
         def to_col(peer):
-            send("col", peer, own.at[step], got_c.at[step, my_col], send_c.at[step], recv_c.at[step, my_col])
+            send(
+                "col", peer, own.at[step], got_c.at[step, my_chip, my_core], send_c.at[step], recv_c.at[step, my_col]
+            )
 
         others(N_ROW, my_row, to_row)
         others(N_CHIP, my_chip, lambda chip: to_col(chip * 2 + my_core))
         to_col(sibling)
-        got_c[step, my_col] = own[step]
+        got_c[step, my_chip, my_core] = own[step]
+        beside()
 
     def forward(step):
         def pass_on(chip):
             slot = chip * 2 + my_core
-            wait_bytes(got_c.at[step, slot], recv_c.at[step, slot])
-            send(
-                "col", sibling, got_c.at[step, slot], got_c.at[step, slot], send_c.at[step], recv_c.at[step, slot]
-            )
+            block = got_c.at[step, chip, my_core]
+            wait_bytes(block, recv_c.at[step, slot])
+            send("col", sibling, block, block, send_c.at[step], recv_c.at[step, slot])
 
         others(N_CHIP, my_chip, pass_on)
 
@@ -339,24 +354,41 @@
         return jnp.concatenate([total[:, 0:K], total[:, K : 2 * K]], axis=0)
 
     def cross_part(step):
-        def dot(chip, carry):
-            slot = chip * 2 + my_core
-            return carry + lax.dot_general(both_c[step, chip], got_c[step, slot], NT, preferred_element_type=F32)
-
-        return lax.fori_loop(0, N_CHIP, dot, jnp.zeros((K, K), F32), unroll=True)
+        total = jnp.zeros((K, K), F32)
+        for side in range(2):
+            core = my_core if side == 0 else 1 - my_core
+            sums = part_c[step, side].reshape(N_CHIP * K, WIDTH)
+            vectors = got_c[step, :, core].reshape(N_CHIP * K, WIDTH)
+            pairs = lax.dot_general(sums, vectors, NT, preferred_element_type=F32)
+            for chip in range(N_CHIP):
+                total += pairs[chip * K : chip * K + K, chip * K : chip * K + K]
+        return total
+
+    def fill_all(step):
+        def enter(chip, carry):
+            for core in range(2):
+                fill_table(got_c.at[step, chip, core], table_c, (chip * 2 + core) * SEGB)
+            return carry
+
+        lax.fori_loop(0, N_CHIP, enter, 0, unroll=4)
 
     def finish_sends(step):
+        sent_c = spare.at[pl.ds(0, N_COL - 1)]
         wait_bytes(got_r.at[step, pl.ds(0, N_ROW - 1)], send_r.at[step])
-        wait_bytes(got_c.at[step, pl.ds(0, N_COL - 1)], send_c.at[step])
+        wait_bytes(sent_c, send_c.at[step])
         wait_bytes(got_r.at[step, pl.ds(0, N_ROW - 1)], send_r.at[2 + step])
-        wait_bytes(got_c.at[step, pl.ds(0, N_COL - 1)], send_c.at[2 + step])
+        wait_bytes(sent_c, send_c.at[2 + step])
         for which in (0, 1) if step == 0 else (2,):
             wait_bytes(gram_r.at[which, pl.ds(0, N_ROW - 1)], send_r.at[4 + which])
             wait_bytes(gram_c.at[which, pl.ds(0, N_COL - 1)], send_c.at[4 + which])
 
-    gather(0)
-    gram_row(0)
-    lax.fori_loop(EARLY_CHUNKS, SLOTS // 64, arrange, 0)
+    def arrange_rest():
+        gram_row(0)
+        lax.fori_loop(EARLY_CHUNKS, SLOTS // 64, arrange, 0)
+
+    gather(0, arrange_rest)
+    for arrival in enter[2:]:
+        arrival.wait()
     for s in range(2):
         columns = jnp.concatenate(
             [col_v[0, :, s * 256 : s * 256 + 256], col_v[0, :, 512 + s * 256 : 768 + s * 256]], axis=1
@@ -367,35 +399,33 @@
         place_r[s * RB : s * RB + RB, :] = jnp.where(hit, 1.0, 0.0).astype(BF16)
     gram_col(0)
 
-    def product(step, while_waiting):
-        def enter_row(peer):
+    def product(step):
+        def arrive_row(peer):
             wait_bytes(got_r.at[step, peer], recv_r.at[step, peer])
+
+        def enter_row(d, carry):
+            peer = lax.rem(my_row + d, N_ROW)
             fill_table(got_r.at[step, peer], table_r, peer * SEGB)
-
-        def enter_same(chip):
-            slot = chip * 2 + my_core
-            fill_table(got_c.at[step, slot], table_c, slot * SEGB)
-
-        def enter_other(chip):
-            slot = chip * 2 + 1 - my_core
-            wait_bytes(got_c.at[step, slot], recv_c.at[step, slot])
-            fill_table(got_c.at[step, slot], table_c, slot * SEGB)
+            return carry
+
+        def arrive_other(chip):
+            wait_bytes(got_c.at[step, chip, 1 - my_core], recv_c.at[step, chip * 2 + 1 - my_core])
 
         fill_table(own.at[step], table_r, my_row * SEGB)
-        others(N_ROW, my_row, enter_row)
+        others(N_ROW, my_row, arrive_row)
+        lax.fori_loop(1, N_ROW, enter_row, 0, unroll=True)
         multiply(row_s, table_r, tiles, prod_c, False, turned if step == 0 else None)
         forward(step)
         add_up(place_c, prod_c, temp, CB)
-        narrow_sums(temp, 1 - my_core, 2, part_c.at[step], N_CHIP)
-        send("col", sibling, part_c.at[step], pair_c.at[step], send_c.at[2 + step], pair_sem.at[step])
-        enter_same(my_chip)
-        others(N_CHIP, my_chip, enter_same)
-        enter_other(my_chip)
-        others(N_CHIP, my_chip, enter_other)
+        narrow_sums(temp, 1 - my_core, 2, part_c.at[step, 1], N_CHIP)
+        send("col", sibling, part_c.at[step, 1], pair_c.at[step], send_c.at[2 + step], pair_sem.at[step])
+        narrow_sums(temp, my_core, 2, part_c.at[step, 0], N_CHIP)
+        arrive_other(my_chip)
+        others(N_CHIP, my_chip, arrive_other)
+        put_gram(1 + step, cross_part(step))
+        gram_row(1 + step)
         wait_bytes(pair_c.at[step], pair_sem.at[step])
         add_pair(temp, my_core, pair_c.at[step], both_c.at[step], N_CHIP)
-        put_gram(1 + step, cross_part(step))
-        gram_row(1 + step)
 
         def sums_to_col(chip):
             send(
@@ -404,6 +434,7 @@
             )
 
         others(N_CHIP, my_chip, sums_to_col)
+        fill_all(step)
         multiply(col_s, table_c, turned, prod_r, True)
         add_up(place_r, prod_r, temp, RB)
         narrow_sums(temp, 0, 1, part_r.at[step], N_ROW)
@@ -416,49 +447,72 @@
             )
 
         others(N_ROW, my_row, sums_to_row)
-        extra = while_waiting()
-        vec_a[...] = both_c[step, my_chip].astype(F32) + part_r[step, my_row].astype(F32)
+        if step == 0:
+            inverse, scale = factor(gram_done(0))
+            norm_inverse = lax.dot_general(
+                inverse * scale, inverse, (((0,), (0,)), ((), ())), precision=HIGHEST, preferred_element_type=F32
+            )
 
         def add_col(chip):
             wait_bytes(sum_c.at[step, chip], recv_sum_c.at[step, chip])
             vec_a[...] += sum_c[step, chip].astype(F32)
 
-        def add_row(peer):
+        vec_a[...] = both_c[step, my_chip].astype(F32) + part_r[step, my_row].astype(F32)
+        others(N_CHIP, my_chip, add_col)
+        half = gram_done(1 + step)
+        cross = half + half.T
+        if step == 0:
+            coupling = jnp.dot(cross, norm_inverse, precision=HIGHEST, preferred_element_type=F32)
+            vec_a[...] -= jnp.dot(coupling, vec_x[...], precision=HIGHEST, preferred_element_type=F32)
+
+        def arrive_sum(peer):
             wait_bytes(sum_r.at[step, peer], recv_sum_r.at[step, peer])
-            vec_a[...] += sum_r[step, peer].astype(F32)
-
-        others(N_CHIP, my_chip, add_col)
-        others(N_ROW, my_row, add_row)
-        half = gram_done(1 + step)
-        return half + half.T, extra
-
-    cross, (inverse, scale) = product(0, lambda: factor(gram_done(0)))
-    halfway = lax.dot_general(inverse, cross, NT, precision=HIGHEST, preferred_element_type=F32) * scale
-    coupling = lax.dot_general(
-        halfway, inverse, (((0,), (0,)), ((), ())), precision=HIGHEST, preferred_element_type=F32
-    )
-    residual = vec_a[...] - jnp.dot(coupling, vec_x[...], precision=HIGHEST, preferred_element_type=F32)
-    own[1] = residual.astype(BF16)
-    gather(1)
-    residual_out[...] = residual
-    finish_sends(0)
-
-    last, _ = product(1, lambda: None)
-    image_out[...] = vec_a[...]
-    gram_out[...] = last * (1.0 / (N_ROW * N_COL * SEGB * TILE))
+
+        others(N_ROW, my_row, arrive_sum)
+        sum_r[step, my_row] = jnp.zeros((K, WIDTH), BF16)
+
+        def add_row(p, carry):
+            total = vec_a[:, lane_block(p)]
+            for slot in range(N_ROW):
+                total += sum_r[step, slot, :, lane_block(p)].astype(F32)
+            vec_a[:, lane_block(p)] = total
+            if step == 0:
+                own[1, :, lane_block(p)] = total.astype(BF16)
+            return carry
+
+        lax.fori_loop(0, 8, add_row, 0, unroll=True)
+        return cross
+
+    product(0)
+
+    def keep_residual():
+        by_vector_to_by_row(vec_a, temp, by_row)
+        by_row_to_flat(by_row, vec_x)
+        leave(0, vec_x, residual_out).start()
+        finish_sends(0)
+
+    gather(1, keep_residual)
+    last = product(1)
+    by_vector_to_by_row(vec_a, temp, by_row)
+    by_row_to_flat(by_row, vec_b)
+    gram_last[...] = last * (1.0 / (N_ROW * N_COL * SEGB * TILE))
+    leave(1, vec_b, image_out).start()
+    leave(2, gram_last, gram_out).start()
     finish_sends(1)
-
-
-def lay_flat(residual, image, gram, residual_out, image_out, gram_out, temp, by_row):
-    for source, target in ((residual, residual_out), (image, image_out)):
-        by_vector_to_by_row(source, temp, by_row)
-        by_row_to_flat(by_row, target)
+    leave(0, vec_x, residual_out).wait()
+    leave(1, vec_b, image_out).wait()
+    leave(2, gram_last, gram_out).wait()
+
+
+def pass_results(residual, image, gram, residual_out, image_out, gram_out):
+    residual_out[...] = residual[...]
+    image_out[...] = image[...]
     gram_out[...] = gram[...]
 
 
 def local(block_x, tile_values, row_block, col_block, tile_counts):
     vmem = pl.BlockSpec(memory_space=pltpu.VMEM)
-    smem = pl.BlockSpec(memory_space=pltpu.SMEM)
+    anywhere = pl.BlockSpec(memory_space=pl.ANY)
     kinds = 7
     vectors = (
         jax.ShapeDtypeStruct((SEGB, WIDTH), F32),
@@ -468,8 +522,8 @@
     results = pl.pallas_call(
         kernel,
         out_shape=vectors,
-        in_specs=[vmem, pl.BlockSpec(memory_space=pl.ANY), smem, smem, smem, vmem, vmem],
-        out_specs=(vmem, vmem, vmem),
+        in_specs=[anywhere] * 5,
+        out_specs=(anywhere,) * 3,
         scratch_shapes=[
             pltpu.VMEM((SLOTS // 64, 4, 16, TILE * TILE), BF16),
             pltpu.VMEM((16 * STAGE_PITCH, 128), F32),
@@ -481,21 +535,33 @@
             pltpu.VMEM((2 * CB, 512), BF16),
             pltpu.VMEM((K * Y_PITCH, 128), F32),
             pltpu.VMEM((K * Y_PITCH, 128), F32),
+            pltpu.VMEM((SEGB, WIDTH), F32),
+            pltpu.SMEM((1, 1, SLOTS), jnp.int32),
+            pltpu.SMEM((1, 1, SLOTS), jnp.int32),
+            pltpu.SMEM((1, 1), jnp.int32),
+            pltpu.VMEM((1, 1, SLOTS), jnp.int32),
+            pltpu.VMEM((1, 1, SLOTS), jnp.int32),
             pltpu.VMEM((N_COL * 128, 128), F32),
+            pltpu.VMEM((128, 128), F32),
             pltpu.VMEM((K, WIDTH), F32),
             pltpu.VMEM((K, WIDTH), F32),
+            pltpu.VMEM((K, WIDTH), F32),
+            pltpu.VMEM((K, K), F32),
             pltpu.VMEM((2, K, WIDTH), BF16),
             pltpu.VMEM((2, N_ROW, K, WIDTH), BF16),
-            pltpu.VMEM((2, N_COL, K, WIDTH), BF16),
+            pltpu.VMEM((2, N_CHIP, 2, K, WIDTH), BF16),
             pltpu.VMEM((2, N_ROW, K, WIDTH), BF16),
+            pltpu.VMEM((2, 2, N_CHIP, K, WIDTH), BF16),
             pltpu.VMEM((2, N_CHIP, K, WIDTH), BF16),
             pltpu.VMEM((2, N_CHIP, K, WIDTH), BF16),
-            pltpu.VMEM((2, N_CHIP, K, WIDTH), BF16),
+            pltpu.VMEM((N_COL, K, WIDTH), BF16),
             pltpu.VMEM((2, N_ROW, K, WIDTH), BF16),
             pltpu.VMEM((2, N_CHIP, K, WIDTH), BF16),
             pltpu.VMEM((6, 8, 128), F32),
             pltpu.VMEM((3, N_ROW, 8, 128), F32),
             pltpu.VMEM((3, N_COL, 8, 128), F32),
+            pltpu.SemaphoreType.DMA((6,)),
+            pltpu.SemaphoreType.DMA((3,)),
             pltpu.SemaphoreType.DMA((SLOTS // 64, 4)),
             pltpu.SemaphoreType.DMA((kinds,)),
             pltpu.SemaphoreType.DMA((kinds,)),
@@ -511,13 +577,9 @@
             collective_id=0, has_side_effects=True, vmem_limit_bytes=58 << 20
         ),
         cost_estimate=pl.CostEstimate(flops=1 << 30, bytes_accessed=9 << 20, transcendentals=0),
-    )(block_x, tile_values, row_block, col_block, tile_counts, row_block, col_block)
+    )(block_x, tile_values, row_block, col_block, tile_counts)
     return pl.pallas_call(
-        lay_flat,
-        out_shape=vectors,
-        in_specs=[vmem] * 3,
-        out_specs=(vmem, vmem, vmem),
-        scratch_shapes=[pltpu.VMEM((128, 128), F32), pltpu.VMEM((128, 128), F32)],
+        pass_results, out_shape=vectors, in_specs=[vmem] * 3, out_specs=(vmem,) * 3
     )(*results)
 
 

time: 63 us -> 59.5 us (0.944)
  Pallas kernels: 61.5 us -> 58.1 us
    pallas_call x2, Pallas kernels: 61.5 us -> 58.1 us  [the longest x1 56.6 us: local(): pl.pallas_call(kernel, out_shape=vectors, in_specs=[anywhere] * 5, out_sp...]
where the time goes in v4:
time: 59.5 us; the launch traced here: 59.4 us
  Pallas kernels  58.1 us (98%)
  between operations  1.29 us (2%)
    pallas_call x1, Pallas kernels, local(): pl.pallas_call(kernel, out_shape=vectors, in_specs=[anywhere] * 5, out_sp...  56.6 us
    pallas_call x1, Pallas kernels, local(): pl.pallas_call(pass_results, out_shape=vectors, in_specs=[vmem] * 3, out_...  1.53 us

profile of v4, /device:TPU:1, one launch (start us, length us, event | category | flops | bytes accessed | tf_op | source)
XLA Modules:
  0.0 59.4 jit_solution(1479535794229145325)
XLA Ops:
  1.3 56.6 %shard_map.76 = (f32[16,1024]{1,0:T(8,128)}, f32[16,1024]{1,0:T(8,128)}, f32[16,16]{1,0:T(8,128)}) custom-call(f32[16,1024]{1,0:T(8,128)} %block_x.1, bf16[1,1,1024,4096]{3,2,1,0:T(8,128)(2,1)} %tile_values.1, s32[1,1,1024]{2,1,0:T(1,128)} %row_block.1, s32[1,1,1024]{2,1,0:T(1,128)} %col_block.1, s32[1,1]{1,0:T(1,128)S(6)} %copy.8.tile_counts), custom_call_target="tpu_custom_call" | custom-call | flops 1073741824 | bytes 9437184 | tf_op jit(solution)/shard_map/pallas_call | solution.py:522
  57.8 1.5 %shard_map.77 = (f32[16,1024]{1,0:T(8,128)}, f32[16,1024]{1,0:T(8,128)}, f32[16,16]{1,0:T(8,128)}) custom-call(f32[16,1024]{1,0:T(8,128)} %get-tuple-element.6.residual, f32[16,1024]{1,0:T(8,128)} %get-tuple-element.7.image, f32[16,16]{1,0:T(8,128)} %get-tuple-element.8.gram), custom_call_target="tpu_custom_call" | custom-call | tf_op jit(solution)/shard_map/pallas_call | solution.py:581

commit v5 on v4

--- a/solution.py
+++ b/solution.py
@@ -22,7 +22,7 @@
 CB = N_COL * SEGB
 STAGE_PITCH = 136
 Y_PITCH = 520
-EARLY_CHUNKS = 8
+EARLY_CHUNKS = 5
 HIGHEST = lax.Precision.HIGHEST
 NT = (((1,), (1,)), ((), ()))
 NN = (((1,), (0,)), ((), ()))
@@ -244,7 +244,7 @@
             use(lax.rem(me + d, size))
             return carry
 
-        lax.fori_loop(1, size, step, 0)
+        lax.fori_loop(1, size, step, 0, unroll=True)
 
     def wait_bytes(block, sem):
         pltpu.make_async_copy(block, block, sem).wait()
@@ -424,6 +424,7 @@
         others(N_CHIP, my_chip, arrive_other)
         put_gram(1 + step, cross_part(step))
         gram_row(1 + step)
+        fill_all(step)
         wait_bytes(pair_c.at[step], pair_sem.at[step])
         add_pair(temp, my_core, pair_c.at[step], both_c.at[step], N_CHIP)
 
@@ -434,11 +435,10 @@
             )
 
         others(N_CHIP, my_chip, sums_to_col)
-        fill_all(step)
         multiply(col_s, table_c, turned, prod_r, True)
+        gram_col(1 + step)
         add_up(place_r, prod_r, temp, RB)
         narrow_sums(temp, 0, 1, part_r.at[step], N_ROW)
-        gram_col(1 + step)
 
         def sums_to_row(peer):
             send(

time: 59.5 us -> 58.3 us (0.980)
  Pallas kernels: 58.1 us -> 56.8 us
    pallas_call x1, Pallas kernels: 56.6 us -> 55.3 us  [local(): pl.pallas_call(kernel, out_shape=vectors, in_specs=[anywhere] * 5, out_sp...]
where the time goes in v5:
time: 58.3 us; the launch traced here: 58.1 us
  Pallas kernels  56.8 us (97%)
  between operations  1.29 us (2%)
    pallas_call x1, Pallas kernels, local(): pl.pallas_call(kernel, out_shape=vectors, in_specs=[anywhere] * 5, out_sp...  55.3 us
    pallas_call x1, Pallas kernels, local(): pl.pallas_call(pass_results, out_shape=vectors, in_specs=[vmem] * 3, out_...  1.53 us

profile of v5, /device:TPU:1, one launch (start us, length us, event | category | flops | bytes accessed | tf_op | source)
XLA Modules:
  0.0 58.1 jit_solution(7492322792448147339)
XLA Ops:
  1.3 55.3 %shard_map.76 = (f32[16,1024]{1,0:T(8,128)}, f32[16,1024]{1,0:T(8,128)}, f32[16,16]{1,0:T(8,128)}) custom-call(f32[16,1024]{1,0:T(8,128)} %block_x.1, bf16[1,1,1024,4096]{3,2,1,0:T(8,128)(2,1)} %tile_values.1, s32[1,1,1024]{2,1,0:T(1,128)} %row_block.1, s32[1,1,1024]{2,1,0:T(1,128)} %col_block.1, s32[1,1]{1,0:T(1,128)S(6)} %copy.8.tile_counts), custom_call_target="tpu_custom_call" | custom-call | flops 1073741824 | bytes 9437184 | tf_op jit(solution)/shard_map/pallas_call | solution.py:522
  56.6 1.5 %shard_map.77 = (f32[16,1024]{1,0:T(8,128)}, f32[16,1024]{1,0:T(8,128)}, f32[16,16]{1,0:T(8,128)}) custom-call(f32[16,1024]{1,0:T(8,128)} %get-tuple-element.6.residual, f32[16,1024]{1,0:T(8,128)} %get-tuple-element.7.image, f32[16,16]{1,0:T(8,128)} %get-tuple-element.8.gram), custom_call_target="tpu_custom_call" | custom-call | tf_op jit(solution)/shard_map/pallas_call | solution.py:581

commit v6 on v5

--- a/solution.py
+++ b/solution.py
@@ -22,7 +22,7 @@
 CB = N_COL * SEGB
 STAGE_PITCH = 136
 Y_PITCH = 520
-EARLY_CHUNKS = 5
+EARLY_CHUNKS = 3
 HIGHEST = lax.Precision.HIGHEST
 NT = (((1,), (1,)), ((), ()))
 NN = (((1,), (0,)), ((), ()))
@@ -299,6 +299,16 @@
         load_groups(raw, stage, tiles, chunk, count)
         return carry
 
+    for arrival in enter[2:]:
+        arrival.wait()
+    for s in range(2):
+        columns = jnp.concatenate(
+            [col_v[0, :, s * 256 : s * 256 + 256], col_v[0, :, 512 + s * 256 : 768 + s * 256]], axis=1
+        )
+        hit = lax.broadcasted_iota(jnp.int32, (CB, 512), 0) == columns
+        place_c[s * CB : s * CB + CB, :] = jnp.where(hit, 1.0, 0.0).astype(BF16)
+        hit = lax.broadcasted_iota(jnp.int32, (RB, 512), 0) == row_v[0, :, s * 512 : s * 512 + 512]
+        place_r[s * RB : s * RB + RB, :] = jnp.where(hit, 1.0, 0.0).astype(BF16)
     lax.fori_loop(0, EARLY_CHUNKS, arrange, 0)
     pl.semaphore_wait(barrier, N_ROW + N_COL - 2)
 
@@ -387,16 +397,6 @@
         lax.fori_loop(EARLY_CHUNKS, SLOTS // 64, arrange, 0)
 
     gather(0, arrange_rest)
-    for arrival in enter[2:]:
-        arrival.wait()
-    for s in range(2):
-        columns = jnp.concatenate(
-            [col_v[0, :, s * 256 : s * 256 + 256], col_v[0, :, 512 + s * 256 : 768 + s * 256]], axis=1
-        )
-        hit = lax.broadcasted_iota(jnp.int32, (CB, 512), 0) == columns
-        place_c[s * CB : s * CB + CB, :] = jnp.where(hit, 1.0, 0.0).astype(BF16)
-        hit = lax.broadcasted_iota(jnp.int32, (RB, 512), 0) == row_v[0, :, s * 512 : s * 512 + 512]
-        place_r[s * RB : s * RB + RB, :] = jnp.where(hit, 1.0, 0.0).astype(BF16)
     gram_col(0)
 
     def product(step):

time: 58.3 us -> 58.3 us (level)
  no operation moved by 1% of the time
where the time goes in v6:
time: 58.3 us; the launch traced here: 58.1 us
  Pallas kernels  56.8 us (97%)
  between operations  1.29 us (2%)
    pallas_call x1, Pallas kernels, local(): pl.pallas_call(kernel, out_shape=vectors, in_specs=[anywhere] * 5, out_sp...  55.3 us
    pallas_call x1, Pallas kernels, local(): pl.pallas_call(pass_results, out_shape=vectors, in_specs=[vmem] * 3, out_...  1.53 us

profile of v6, /device:TPU:1, one launch (start us, length us, event | category | flops | bytes accessed | tf_op | source)
XLA Modules:
  0.0 58.1 jit_solution(11260085938856752290)
XLA Ops:
  1.3 55.3 %shard_map.76 = (f32[16,1024]{1,0:T(8,128)}, f32[16,1024]{1,0:T(8,128)}, f32[16,16]{1,0:T(8,128)}) custom-call(f32[16,1024]{1,0:T(8,128)} %block_x.1, bf16[1,1,1024,4096]{3,2,1,0:T(8,128)(2,1)} %tile_values.1, s32[1,1,1024]{2,1,0:T(1,128)} %row_block.1, s32[1,1,1024]{2,1,0:T(1,128)} %col_block.1, s32[1,1]{1,0:T(1,128)S(6)} %copy.8.tile_counts), custom_call_target="tpu_custom_call" | custom-call | flops 1073741824 | bytes 9437184 | tf_op jit(solution)/shard_map/pallas_call | solution.py:522
  56.6 1.5 %shard_map.77 = (f32[16,1024]{1,0:T(8,128)}, f32[16,1024]{1,0:T(8,128)}, f32[16,16]{1,0:T(8,128)}) custom-call(f32[16,1024]{1,0:T(8,128)} %get-tuple-element.6.residual, f32[16,1024]{1,0:T(8,128)} %get-tuple-element.7.image, f32[16,16]{1,0:T(8,128)} %get-tuple-element.8.gram), custom_call_target="tpu_custom_call" | custom-call | tf_op jit(solution)/shard_map/pallas_call | solution.py:581

commit v7 on v6

--- a/solution.py
+++ b/solution.py
@@ -154,7 +154,7 @@
             products[pl.ds(8 * Y_PITCH + place, 8, stride=Y_PITCH), :] = merged[8:]
         return carry
 
-    lax.fori_loop(0, GROUPS, step, 0, unroll=128)
+    lax.fori_loop(0, GROUPS, step, 0, unroll=True)
 
 
 def add_up(places, products, temp, blocks):

time: 58.3 us -> 57.7 us (0.990)
  no operation moved by 1% of the time
where the time goes in v7:
time: 57.7 us; the launch traced here: 57.5 us
  Pallas kernels  56.3 us (98%)
  between operations  1.29 us (2%)
    pallas_call x1, Pallas kernels, local(): pl.pallas_call(kernel, out_shape=vectors, in_specs=[anywhere] * 5, out_sp...  54.7 us
    pallas_call x1, Pallas kernels, local(): pl.pallas_call(pass_results, out_shape=vectors, in_specs=[vmem] * 3, out_...  1.53 us

profile of v7, /device:TPU:1, one launch (start us, length us, event | category | flops | bytes accessed | tf_op | source)
XLA Modules:
  0.0 57.5 jit_solution(15784542863704546963)
XLA Ops:
  1.3 54.7 %shard_map.76 = (f32[16,1024]{1,0:T(8,128)}, f32[16,1024]{1,0:T(8,128)}, f32[16,16]{1,0:T(8,128)}) custom-call(f32[16,1024]{1,0:T(8,128)} %block_x.1, bf16[1,1,1024,4096]{3,2,1,0:T(8,128)(2,1)} %tile_values.1, s32[1,1,1024]{2,1,0:T(1,128)} %row_block.1, s32[1,1,1024]{2,1,0:T(1,128)} %col_block.1, s32[1,1]{1,0:T(1,128)S(6)} %copy.8.tile_counts), custom_call_target="tpu_custom_call" | custom-call | flops 1073741824 | bytes 9437184 | tf_op jit(solution)/shard_map/pallas_call | solution.py:522
  56.0 1.5 %shard_map.77 = (f32[16,1024]{1,0:T(8,128)}, f32[16,1024]{1,0:T(8,128)}, f32[16,16]{1,0:T(8,128)}) custom-call(f32[16,1024]{1,0:T(8,128)} %get-tuple-element.6.residual, f32[16,1024]{1,0:T(8,128)} %get-tuple-element.7.image, f32[16,16]{1,0:T(8,128)} %get-tuple-element.8.gram), custom_call_target="tpu_custom_call" | custom-call | tf_op jit(solution)/shard_map/pallas_call | solution.py:581
